TPU v7x, 512 devices: a whole 4x8x8 slice. The times are simulated.
512 devices in a mesh: cells: 64 (over x, z, core), grp: 8 (over y).
Axes of the slice: x: 4, y: 8, z: 8, core: 2. Of those that a mesh axis runs over, the one named last changes fastest.
Arguments:
- ensemble: float32 [128, 262144], P('grp', 'cells'), may hold values from -6 to 6
- gauge_owner: int32 [2, 512, 1], replicated, may hold values from 0 to 63; in each aligned block of 512 rows (0 to 511, 512 to 1023, ..., all dimensions but the last counted through in order) at most 24 rows name the same one
- gauge_block: int32 [2, 512], replicated, may hold values from 0 to 31
- gauge_weight: float32 [2, 512, 128], replicated, may hold values from -0.5 to 0.5
- gauge_value: float32 [2, 512], replicated, may hold values from -6 to 6
- gauge_error: float32 [2, 512], replicated, may hold values from 0.5 to 4
- loc_level: int32 [2, 2048], P(None, 'cells'), may hold values from 0 to 4
Outputs:
- analysis: float32 [128, 262144], P('grp', 'cells')
Inputs may be any that keep to these rules, and one draw needn't show every extreme that they name: `gauge_owner`: in each batch no index of cells owns more than 24 gauges, and some index owns exactly 24.
All inputs are finite; a program needn't handle non-finite values.
Results may differ from a plain program's by a relative error of at most 0.0001.
Values sent between devices are 32-bit elements; how exact they have to be, the bound alone decides.
A program may use at most 64 MiB of HBM per device.

v0:
```python
import jax
import jax.numpy as jnp
from jax import lax
from jax.sharding import PartitionSpec as P

NBATCH = 2
NSIT = 12
CAP = 24


def make_transform(gram, bvec):
    order = gram.shape[0]
    identity = jnp.eye(order, dtype=jnp.float32)
    amat = identity + gram
    lower = jnp.linalg.cholesky(amat)
    middle = lax.linalg.triangular_solve(lower, bvec[:, None], left_side=True, lower=True)
    wbar = lax.linalg.triangular_solve(lower, middle, left_side=True, lower=True, transpose_a=True)[
        :, 0
    ]
    scal = jnp.trace(amat)

    def newton(index, carry):
        ymat, zmat = carry
        qmat = 1.5 * identity - 0.5 * jnp.dot(zmat, ymat, precision=lax.Precision.HIGHEST)
        return (
            jnp.dot(ymat, qmat, precision=lax.Precision.HIGHEST),
            jnp.dot(qmat, zmat, precision=lax.Precision.HIGHEST),
        )

    ymat, zmat = lax.fori_loop(0, NSIT, newton, (amat / scal, identity))
    sqinv = zmat / jnp.sqrt(scal)
    return sqinv + wbar[:, None] / jnp.sqrt(jnp.float32(order - 1)) - identity


def local(ensemble, gauge_owner, gauge_block, gauge_weight, gauge_value, gauge_error, loc_level):
    groups = lax.axis_size("grp")
    local_members = ensemble.shape[0]
    all_members = local_members * groups
    cells_local = ensemble.shape[1]
    block_len = gauge_weight.shape[2]
    blocks_local = cells_local // block_len
    owner_index = lax.axis_index("cells")
    group_index = lax.axis_index("grp")
    scale = jnp.sqrt(jnp.float32(all_members - 1))
    slot_ids = jnp.arange(CAP, dtype=jnp.int32)
    state = ensemble
    for batch in range(NBATCH):
        owned = gauge_owner[batch, :, 0] == owner_index
        ranking = jnp.cumsum(owned.astype(jnp.int32)) - 1
        chosen = owned[None, :] & (ranking[None, :] == slot_ids[:, None])
        chosen_f = chosen.astype(jnp.float32)
        live = jnp.sum(chosen_f, axis=1)
        slot_block = jnp.sum(jnp.where(chosen, gauge_block[batch][None, :], 0), axis=1)
        slot_weight = jnp.dot(chosen_f, gauge_weight[batch], precision=lax.Precision.HIGHEST)
        slot_value = jnp.dot(chosen_f, gauge_value[batch], precision=lax.Precision.HIGHEST)
        slot_error = jnp.dot(chosen_f, gauge_error[batch], precision=lax.Precision.HIGHEST) + (
            1.0 - live
        )
        blocked = state.reshape(local_members, blocks_local, block_len)
        picked = blocked[:, slot_block, :]
        partial_prior = jnp.einsum(
            "msc,sc->ms", picked, slot_weight, precision=lax.Precision.HIGHEST
        )
        prior = lax.all_gather(partial_prior, "grp", axis=0, tiled=True)
        ymean = jnp.mean(prior, axis=0)
        smat = ((prior - ymean[None, :]) / (slot_error[None, :] * scale)).T * live[:, None]
        dvec = (slot_value - ymean) / slot_error * live
        empty = (
            jnp.zeros((all_members, all_members), jnp.float32),
            jnp.zeros((all_members,), jnp.float32),
        )
        s_piece = lax.all_gather(smat, "cells", axis=0, tiled=True)
        d_piece = lax.all_gather(dvec, "cells", axis=0, tiled=True)
        gram = empty[0] + jnp.dot(s_piece.T, s_piece, precision=lax.Precision.HIGHEST)
        bvec = empty[1] + jnp.dot(s_piece.T, d_piece, precision=lax.Precision.HIGHEST)
        mixer = make_transform(gram, bvec)
        levels = loc_level[batch].astype(jnp.float32) / 4.0
        taper = jnp.repeat(levels, block_len)
        columns = lax.dynamic_slice_in_dim(mixer, group_index * local_members, local_members, 1)
        column_total = jnp.sum(columns, axis=0)
        piece = lax.all_gather(state, "grp", axis=0, tiled=True)
        accum = jnp.zeros((local_members, cells_local), jnp.float32)
        totals = jnp.zeros((cells_local,), jnp.float32)
        mix_rows = lax.slice_in_dim(columns, 0, piece.shape[0], axis=0)
        accum, totals = (
            accum + jnp.dot(mix_rows.T, piece, precision=lax.Precision.HIGHEST),
            totals + jnp.sum(piece, axis=0),
        )
        mixed = accum - column_total[:, None] * (totals / all_members)[None, :]
        state = state + taper[None, :] * mixed
    return state


def solution(mesh):
    placed = (P("grp", "cells"), P(), P(), P(), P(), P(), P(None, "cells"))
    return jax.shard_map(
        local, mesh=mesh, in_specs=placed, out_specs=P("grp", "cells"), check_vma=False
    )
```

profile of v0, /device:TPU:1, one launch (start us, length us, event | category | flops | bytes accessed | tf_op | source)
XLA Modules:
  0.0 519.5 jit_solution(13977650407085734264)
XLA Ops:
  6.5 0.7 all-gather.3.cloned.1.call-update
  7.3 1.0 copy_bitcast_fusion.1
  8.3 0.7 compare_reduce_fusion
  9.0 0.3 reduce-window.16
  9.6 0.8 fusion.73
  10.7 1.2 fusion.26
  11.8 0.6 gather_fusion
  12.4 0.4 fusion.32
  12.9 21.0 %all_gather.24 = f32[128,24]{1,0:T(8,128)S(1)} all-gather(f32[16,24]{1,0:T(8,128)S(1)} %bitcast.237), channel_id=1, replica_groups=mesh['cells'=64,'grp'=8] {'grp'}, dimensions={0}, use_global_device_ids=true | all-gather | bytes 13824 | tf_op jit(solution)/shard_map/all_gather | solution.py:64
  34.0 0.8 broadcast_multiply_fusion.3
  34.9 63.1 %all_gather.25 = f32[1536,128]{1,0:T(8,128)S(1)} all-gather(f32[24,128]{1,0:T(8,128)S(1)} %multiply_bitcast_fusion.1), channel_id=1, replica_groups=mesh['cells'=64,'grp'=8] {'cells'}, dimensions={0}, use_global_device_ids=true | all-gather | bytes 798720 | tf_op jit(solution)/shard_map/all_gather | solution.py:72
  98.1 2.0 select_reduce_fusion.3
  100.2 0.7 broadcast_divide_fusion.1
  100.9 9.8 %while.26 = (s32[]{:T(128)}, f32[128,128]{0,1:T(8,128)S(1)}, f32[128,128]{1,0:T(8,128)S(1)}, s32[]{:T(128)}) while((s32[]{:T(128)}, f32[128,128]{0,1:T(8,128)S(1)}, f32[128,128]{1,0:T(8,128)S(1)}, s32[]{:T(128)}) %tuple.63), condition=%wide.region_7.8_spmd.clone, body=%wide.region_6.7_spmd.clone.sunk | while | flops 75563008 | bytes 852021 | solution.py:30
  102.2 0.3 convolution_bitcast_fusion.14
  103.1 0.3 convolution_bitcast_fusion.14
  103.9 0.3 convolution_bitcast_fusion.14
  104.7 0.3 convolution_bitcast_fusion.14
  105.5 0.3 convolution_bitcast_fusion.14
  106.3 0.3 convolution_bitcast_fusion.14
  107.1 0.3 convolution_bitcast_fusion.14
  108.0 0.3 convolution_bitcast_fusion.14
  108.8 0.3 convolution_bitcast_fusion.14
  109.6 0.3 convolution_bitcast_fusion.14
  110.4 0.3 convolution_bitcast_fusion.14
  111.7 11.7 %cholesky.44 = f32[128,128]{1,0:T(8,128)S(1)} custom-call(f32[128,128]{1,0:T(8,128)S(1)} %fusion.41), custom_call_target="Cholesky" | custom-call | tf_op jit(solution)/shard_map/jit(cholesky)/cholesky | solution.py:15
  123.4 0.6 compare_reduce_fusion.3
  124.1 0.7 fusion.34
  124.7 9.8 %custom-call.11 = f32[1,128,128]{1,2,0:T(8,128)S(1)} custom-call(f32[1,128,128]{2,1,0:T(8,128)S(1)} %fusion.34), custom_call_target="InvertDiagBlocksLowerTriangular" | custom-call | tf_op jit(solution)/shard_map/triangular_solve/custom-call.2 | solution.py:17
  134.6 1.3 dynamic-slice
  136.9 125.7 %all-reduce = f32[1536]{0:T(1024)S(1)} all-reduce(f32[1536]{0:T(1024)S(1)} %dynamic-update-slice.2), channel_id=1, replica_groups=mesh['cells'=64,'grp'=8] {'cells'}, use_global_device_ids=true, to_apply=%add | all-reduce | flops 1536 | bytes 12288
  262.6 0.3 reduce-window.24
  263.4 0.5 convolution_bitcast_fusion.11
  265.2 1.9 reduce_sum.116
  267.0 0.3 copy-done
  267.4 1.1 fusion.9
  268.5 0.7 copy-done.2
  269.2 0.6 gather_fusion.1
  269.8 0.4 fusion.30
  270.3 19.7 %all_gather.28 = f32[128,24]{1,0:T(8,128)S(1)} all-gather(f32[16,24]{1,0:T(8,128)S(1)} %bitcast.238), channel_id=1, replica_groups=mesh['cells'=64,'grp'=8] {'grp'}, dimensions={0}, use_global_device_ids=true | all-gather | bytes 13824 | tf_op jit(solution)/shard_map/all_gather | solution.py:64
  290.2 55.2 %all_gather.29 = f32[1536,128]{1,0:T(8,128)S(1)} all-gather(f32[24,128]{1,0:T(8,128)S(1)} %multiply_bitcast_fusion), channel_id=1, replica_groups=mesh['cells'=64,'grp'=8] {'cells'}, dimensions={0}, use_global_device_ids=true | all-gather | bytes 798720 | tf_op jit(solution)/shard_map/all_gather | solution.py:72
  345.4 2.0 select_reduce_fusion.2
  347.4 0.6 broadcast_divide_fusion
  348.1 9.8 %while.27 = (s32[]{:T(128)}, f32[128,128]{0,1:T(8,128)S(1)}, f32[128,128]{1,0:T(8,128)S(1)}, s32[]{:T(128)}) while((s32[]{:T(128)}, f32[128,128]{0,1:T(8,128)S(1)}, f32[128,128]{1,0:T(8,128)S(1)}, s32[]{:T(128)}) %tuple.66), condition=%wide.region_19.23_spmd.clone, body=%wide.region_18.22_spmd.clone.sunk | while | flops 75563008 | bytes 852021 | solution.py:30
  348.6 0.3 convolution_bitcast_fusion.15
  349.4 0.3 convolution_bitcast_fusion.15
  350.2 0.3 convolution_bitcast_fusion.15
  351.0 0.3 convolution_bitcast_fusion.15
  351.9 0.3 convolution_bitcast_fusion.15
  352.7 0.3 convolution_bitcast_fusion.15
  353.5 0.3 convolution_bitcast_fusion.15
  354.3 0.3 convolution_bitcast_fusion.15
  355.1 0.3 convolution_bitcast_fusion.15
  355.9 0.3 convolution_bitcast_fusion.15
  357.6 0.3 convolution_bitcast_fusion.15
  358.8 11.7 %cholesky.55 = f32[128,128]{1,0:T(8,128)S(1)} custom-call(f32[128,128]{1,0:T(8,128)S(1)} %fusion.38), custom_call_target="Cholesky" | custom-call | tf_op jit(solution)/shard_map/jit(cholesky)/cholesky | solution.py:15
  370.5 0.6 compare_reduce_fusion.2
  371.2 0.6 fusion.35
  371.8 9.8 %custom-call.13 = f32[1,128,128]{1,2,0:T(8,128)S(1)} custom-call(f32[1,128,128]{2,1,0:T(8,128)S(1)} %fusion.35), custom_call_target="InvertDiagBlocksLowerTriangular" | custom-call | tf_op jit(solution)/shard_map/triangular_solve/custom-call.2 | solution.py:17
  382.0 125.6 %all-reduce.1 = f32[1536]{0:T(1024)S(1)} all-reduce(f32[1536]{0:T(1024)S(1)} %dynamic-update-slice.3), channel_id=1, replica_groups=mesh['cells'=64,'grp'=8] {'cells'}, use_global_device_ids=true, to_apply=%add.1 | all-reduce | flops 1536 | bytes 12288
  507.6 0.5 convolution_bitcast_fusion.8
  508.7 1.9 reduce_sum.123
  510.5 0.3 copy-done.1
  510.9 1.8 fusion.7
  (177 shorter events, 16.9 us)
Async XLA Ops:
  6.5 258.6 %all-gather.3.cloned.1.call-start = ((), (), s32[]{:S(2)}) async-start(), calls=%async_computation | async-start | bytes 2359296 | tf_op jit(solution)/shard_map/all_gather | solution.py:81
  7.3 501.4 %all-gather.5.cloned.1.call-start = ((), (), s32[]{:S(2)}) async-start(), calls=%async_computation.1 | async-start | bytes 2359296 | tf_op jit(solution)/shard_map/all_gather | solution.py:81
  100.9 35.6 %copy-start.8 = (f32[2,512]{1,0:T(2,128)S(1)}, f32[2,512]{1,0:T(2,128)}, u32[]{:S(2)}) copy-start(f32[2,512]{1,0:T(2,128)} %param.20) | copy-start | bytes 12292
  100.9 163.7 %copy-start.6 = (s32[2,32]{1,0:T(2,128)S(1)}, s32[2,32]{1,0:T(2,128)}, u32[]{:S(2)}) copy-start(s32[2,32]{1,0:T(2,128)} %param.22) | copy-start | bytes 772
  100.9 163.7 %copy-start.7 = (f32[2,512]{1,0:T(2,128)S(1)}, f32[2,512]{1,0:T(2,128)}, u32[]{:S(2)}) copy-start(f32[2,512]{1,0:T(2,128)} %param.21) | copy-start | bytes 12292
  100.9 164.0 %copy-start.5 = (f32[2,512,128]{2,1,0:T(8,128)S(1)}, f32[2,512,128]{2,1,0:T(8,128)}, u32[]{:S(2)}) copy-start(f32[2,512,128]{2,1,0:T(8,128)} %param.19) | copy-start | bytes 1572868
  110.8 156.2 %copy-start.4 = (f32[16,4096]{1,0:T(8,128)S(1)}, f32[16,4096]{1,0:T(8,128)}, u32[]{:S(2)}) copy-start(f32[16,4096]{1,0:T(8,128)} %param.16) | copy-start | bytes 786436
  265.1 2.2 copy-start
  268.5 0.7 copy-start.2
  357.9 152.6 %copy-start.3 = (f32[16,4096]{1,0:T(8,128)S(1)}, f32[16,4096]{1,0:T(8,128)}, u32[]{:S(2)}) copy-start(f32[16,4096]{1,0:T(8,128)} %copy-done.2) | copy-start | bytes 786436
  508.6 2.2 copy-start.1
Sparse Core Ops, SparseCore 0:
  9.4 45.5 all-gather.2
  269.3 34.8 all-gather.4
where the time goes:
time: 521 us; the launch traced here: 520 us
  blocking collectives  410 us (79%)
  other arithmetic  53.4 us (10%)
  matrix products  30.3 us (6%)
  between operations  15.9 us (3%)
  local copies, waits for them, and re-layouts  7.59 us (1%)
    unnamed x2, blocking collectives  251 us
    all_gather x2, blocking collectives, local(): s_piece = lax.all_gather(smat, 'cells', axis=0, tiled=True)  118 us
    all_gather x2, blocking collectives, local(): prior = lax.all_gather(partial_prior, 'grp', axis=0, tiled=True)  40.7 us
    another operation x6, other arithmetic, make_transform(): lower = jnp.linalg.cholesky(amat)  24.8 us
    another operation x4, other arithmetic, make_transform(): lax.linalg.triangular_solve(lower, middle, left_side=True, lower=True, tr...  20.9 us
  transfers between devices with their start and end apart: 2, of which 0 were waited for; matrix products, arithmetic and copies ran while one was open for 16% of the time, Pallas kernels for 0%

commit v1 on v0

v1 whole, which is shorter than its diff:
```python
import functools

import jax
import jax.numpy as jnp
from jax import lax
from jax.experimental import pallas as pl
from jax.experimental.pallas import tpu as pltpu
from jax.sharding import PartitionSpec as P

MESH = pl.DeviceIdType.MESH
F32, BF16, I32 = jnp.float32, jnp.bfloat16, jnp.int32
NBATCH = 2
NSIT = 12
CAP = 24
NX, NZ, NCORE = 4, 8, 2
NY = 8
NXC = NX * NCORE


def split2(x):
    hi = x.astype(BF16)
    lo = (x - hi.astype(F32)).astype(BF16)
    return hi, lo


def split3(x):
    hi = x.astype(BF16)
    rest = x - hi.astype(F32)
    mid = rest.astype(BF16)
    lo = (rest - mid.astype(F32)).astype(BF16)
    return hi, mid, lo


def nn(a, b):
    return lax.dot_general(a, b, (((1,), (0,)), ((), ())), preferred_element_type=F32)


def nt(a, b):
    return lax.dot_general(a, b, (((1,), (1,)), ((), ())), preferred_element_type=F32)


def iota(shape, dim):
    return lax.broadcasted_iota(I32, shape, dim)


def mm(a, b):
    n = a.shape[0]
    ah, al = split2(a)
    bh, bl = split2(b)
    left = jnp.concatenate([ah, al], axis=1)
    row = jnp.concatenate([bh, bl], axis=1)
    both = nn(left, jnp.concatenate([row, row], axis=0))
    return both[:, :n] + both[:, n:]


def wide(a, x):
    ah, al = split2(a)
    xh, xl = split2(x)
    left = jnp.concatenate([ah, al], axis=1)
    return nn(left, jnp.concatenate([xh, xh], axis=0)) + nn(ah, xl)


def ranks(o_row):
    count = o_row.shape[1]
    o_col = jnp.transpose(jnp.broadcast_to(o_row, (128, count)))
    tiles = []
    for t in range(count // 128):
        same = o_col == o_row[:, t * 128 : (t + 1) * 128]
        earlier = iota((count, 128), 0) > iota((count, 128), 1) + t * 128
        tiles.append(jnp.where(same & earlier, 1.0, 0.0).astype(BF16))
    equal = jnp.concatenate(tiles, axis=1)
    rank_col = nn(equal, jnp.ones((count, 128), BF16))
    rank_row = nt(jnp.ones((8, count), BF16), equal)[0:1]
    return o_col, rank_col, rank_row


def compact(grid3, o_col, rank_col, batch, members):
    count = o_col.shape[0]
    o = o_col.astype(I32)
    r = rank_col.astype(I32)
    tile = ((o >> 4) * NCORE + (o & 1)) * NZ + ((o >> 1) & (NZ - 1))
    row = tile * 8 + 3 * batch + (r >> 3)
    rows_all = grid3.shape[0]
    lanes = iota((count, 128), 1)
    onehot = jnp.concatenate(
        [jnp.where(row == lanes + t * 128, 1.0, 0.0).astype(BF16) for t in range(rows_all // 128)],
        axis=1,
    )
    picked = nn(onehot, grid3)
    keep = (lanes >> 4) == (r & 7)
    kept = jnp.concatenate(
        [jnp.where(keep, picked[:, t * 128 : (t + 1) * 128], 0.0).astype(BF16) for t in range(3)],
        axis=1,
    )
    fold = jnp.where((iota((members, 384), 1) & 15) == iota((members, 384), 0), 1.0, 0.0)
    return nt(fold.astype(BF16), kept)


def gauge_taper(levels, o_row, b_row):
    count = o_row.shape[1]
    i = iota((NXC * NZ, count), 0)
    xc, z = i >> 3, i & (NZ - 1)
    owner = ((xc >> 1) * NZ + z) * NCORE + (xc & 1)
    onehot = jnp.where(owner == o_row, 1.0, 0.0).astype(BF16)
    by_block = nn(jnp.transpose(levels).astype(BF16), onehot)
    hit = iota(by_block.shape, 0) == b_row
    return jnp.sum(jnp.where(hit, by_block, 0.0), axis=0, keepdims=True)


def innovations(prior, value, error):
    members = prior.shape[0]
    ymean = jnp.sum(prior, axis=0, keepdims=True) / members
    smat = (prior - ymean) * (1.0 / (error * jnp.sqrt(jnp.float32(members - 1))))
    dvec = (value - ymean) / error
    sh, sl = split2(smat)
    both = jnp.concatenate([sh, sl], axis=0)
    top = nt(sh, both)
    low = nt(sl, both)
    gram = top[:, :members] + (top[:, members:] + low[:, :members]) + low[:, members:]
    bvec = jnp.sum(smat * dvec, axis=1, keepdims=True)
    return gram, bvec


def inverse_root(amat, eye):
    scal = jnp.sum(jnp.sum(amat * eye, axis=1, keepdims=True), axis=0, keepdims=True)

    def newton(_, carry):
        y, z = carry
        q = 1.5 * eye - 0.5 * mm(z, y)
        return mm(y, q), mm(q, z)

    _, z = lax.fori_loop(0, NSIT, newton, (amat / scal, eye))
    return z * lax.rsqrt(scal)


def eliminate(m_ref, amat):
    n = amat.shape[0]
    m_ref[...] = amat
    lane = iota((1, n), 1)
    lanes = iota((n, n), 1)

    def step(index, carry):
        j = 2 * index
        m = m_ref[...]
        r0 = m_ref[pl.ds(j, 1), :]
        r1 = m_ref[pl.ds(j + 1, 1), :]
        at0, at1 = lane == j, lane == j + 1
        a = jnp.sum(jnp.where(at0, r0, 0.0), axis=1, keepdims=True)
        b = jnp.sum(jnp.where(at1, r0, 0.0), axis=1, keepdims=True)
        c = jnp.sum(jnp.where(at1, r1, 0.0), axis=1, keepdims=True)
        c0 = jnp.sum(jnp.where(lanes == j, m, 0.0), axis=1, keepdims=True)
        c1 = jnp.sum(jnp.where(lanes == j + 1, m, 0.0), axis=1, keepdims=True)
        inv_a = 1.0 / a
        ratio = b * inv_a
        inv_d = 1.0 / (c - b * ratio)
        p11 = inv_d
        p01 = -ratio * inv_d
        p00 = inv_a + ratio * ratio * inv_d
        pivot = at0 | at1
        s1 = (r1 - ratio * r0) * inv_d
        u1 = jnp.where(at0, -p01, jnp.where(at1, -p11, s1))
        u0 = jnp.where(at0, -p00, jnp.where(at1, -p01, r0 * inv_a - ratio * s1))
        m_ref[...] = jnp.where((lanes == j) | (lanes == j + 1), 0.0, m) - c0 * u0 - c1 * u1
        m_ref[pl.ds(j, 1), :] = u0
        m_ref[pl.ds(j + 1, 1), :] = u1
        return carry

    lax.fori_loop(0, n // 2, step, 0)


def apply_mix(dmat, wbar, x, taper):
    members = x.shape[0]
    anomaly = x - jnp.sum(x, axis=0, keepdims=True) / members
    shift = jnp.sum(wbar * anomaly, axis=0, keepdims=True) / jnp.sqrt(jnp.float32(members - 1))
    return x + taper * (wide(dmat, anomaly) + shift)


def kernel(
    ens_ref, own_ref, blk_ref, gw_ref, val_ref, err_ref, lvl_ref, out_ref,
    w_ref, b_ref, y_ref, tile_ref, line_ref, grid_ref, prior_ref, full_ref, res_ref, m_ref,
    s1s, s1r, s2s, s2r, s3s, s3r, s4s, s4r, s5s, s5r,
):
    members = ens_ref.shape[0]
    gauges = own_ref.shape[1]
    cell = lax.axis_index("cells")
    my = lax.axis_index("grp")
    core = cell % NCORE
    mz = (cell // NCORE) % NZ
    mx = cell // (NCORE * NZ)
    mxc = mx * NCORE + core

    def z_peer(d):
        return ((mx * NZ + (mz + d) % NZ) * NCORE + core, my)

    def xc_peer(d):
        xc = (mxc + d) % NXC
        return (((xc // NCORE) * NZ + mz) * NCORE + xc % NCORE, my)

    def y_peer(d):
        return (cell, (my + d) % NY)

    barrier = pltpu.get_barrier_semaphore()
    for d in range(1, 8):
        for peer in (z_peer(d), xc_peer(d), y_peer(d)):
            pl.semaphore_signal(barrier, inc=1, device_id=peer, device_id_type=MESH)

    meta = [ranks(own_ref[b : b + 1, :].astype(F32)) for b in range(NBATCH)]
    slot = iota((CAP, gauges), 0)
    for b in range(NBATCH):
        o_row = own_ref[b : b + 1, :]
        mine = (o_row == cell) & (meta[b][2].astype(I32) == slot)
        pick = jnp.where(mine, 1.0, 0.0).astype(BF16)
        g0, g1, g2 = split3(gw_ref[b])
        w_ref[b * CAP : (b + 1) * CAP, :] = nn(pick, g0) + nn(pick, g1) + nn(pick, g2)
        blocks = jnp.broadcast_to(blk_ref[b : b + 1, :], (128, gauges)).astype(F32).astype(BF16)
        b_ref[b * CAP : (b + 1) * CAP, :] = nt(pick, blocks)

    nblk = ens_ref.shape[1] // 128

    def reading(s, carry):
        want = b_ref[pl.ds(s, 1), :]
        got = jnp.zeros((members, 128), F32)
        for k in range(nblk):
            got = jnp.where(want == k, ens_ref[:, k * 128 : (k + 1) * 128], got)
        y_ref[pl.ds(pl.multiple_of(s * members, members), members), :] = got * w_ref[pl.ds(s, 1), :]
        return carry

    lax.fori_loop(0, NBATCH * CAP, reading, 0)
    y3 = jnp.concatenate(split3(y_ref[...]), axis=1)
    flat = nt(jnp.ones((8, y3.shape[1]), BF16), y3)
    sub = iota((8, 128), 0)
    lane = iota((8, 128), 1)
    tile = jnp.zeros((8, 128), F32)
    for r in range(6):
        tile = jnp.where(sub == r, flat[:, r * 128 : (r + 1) * 128], tile)
    for k in range(nblk):
        level = lvl_ref[0, k].astype(F32) * 0.25
        tile = jnp.where((sub == 6) & (lane == k), level, tile)
    tile_ref[...] = tile

    pl.semaphore_wait(barrier, 21)

    def remote(src, dst, send, recv, peer):
        return pltpu.make_async_remote_copy(
            src_ref=src, dst_ref=dst, send_sem=send, recv_sem=recv,
            device_id=peer, device_id_type=MESH,
        )

    chunk = ens_ref.shape[1] // NY

    def rows(y):
        return pl.ds(pl.multiple_of(y * members, members), members)

    def cols(y):
        return pl.ds(pl.multiple_of(y * chunk, chunk), chunk)

    c1 = [
        remote(tile_ref, line_ref.at[mz], s1s.at[d - 1], s1r.at[d - 1], z_peer(d))
        for d in range(1, NZ)
    ]
    for c in c1:
        c.start()
    line_ref[mz] = tile
    c4 = [
        remote(
            ens_ref.at[:, cols((my + d) % NY)], full_ref.at[rows(my)],
            s4s.at[d - 1], s4r.at[d - 1], y_peer(d),
        )
        for d in range(1, NY)
    ]
    for c in c4:
        c.start()
    full_ref[rows(my), :] = ens_ref[:, cols(my)]
    for c in c1:
        c.wait_recv()
    c2 = [
        remote(line_ref, grid_ref.at[mxc], s2s.at[d - 1], s2r.at[d - 1], xc_peer(d))
        for d in range(1, NXC)
    ]
    for c in c2:
        c.start()
    grid_ref[mxc] = line_ref[...]
    for c in c2:
        c.wait_recv()

    grid3 = jnp.concatenate(split3(grid_ref[...].reshape(NXC * NZ * 8, 128)), axis=1)
    c3 = []
    for b in range(NBATCH):
        prior_ref[b, rows(my), :] = compact(grid3, meta[b][0], meta[b][1], b, members)
        c3.append([
            remote(
                prior_ref.at[b, rows(my)], prior_ref.at[b, rows(my)],
                s3s.at[b, d - 1], s3r.at[b, d - 1], y_peer(d),
            )
            for d in range(1, NY)
        ])
        for c in c3[b]:
            c.start()
    levels = grid_ref[:, :, 6, :].reshape(NXC * NZ, 128)
    taper_g = gauge_taper(levels, own_ref[1:2, :], blk_ref[1:2, :])

    def cell_taper(b):
        each = [
            jnp.full((1, 128), lvl_ref[b, my * (chunk // 128) + k].astype(F32) * 0.25, F32)
            for k in range(chunk // 128)
        ]
        return jnp.concatenate(each, axis=1)

    total = members * NY
    eye = jnp.where(iota((total, total), 0) == iota((total, total), 1), 1.0, 0.0)
    for b in range(NBATCH):
        if b == 0:
            for c in c3[0]:
                c.wait_recv()
            prior = prior_ref[0]
        gram, bvec = innovations(prior, val_ref[b : b + 1, :], err_ref[b : b + 1, :])
        amat = eye + gram
        dmat = inverse_root(amat, eye) - eye
        eliminate(m_ref, amat)
        b_row = jnp.sum(eye * bvec, axis=0, keepdims=True)
        wbar = -jnp.sum(m_ref[...] * b_row, axis=1, keepdims=True)
        if b == 0:
            for c in c3[1]:
                c.wait_recv()
            prior = apply_mix(dmat, wbar, prior_ref[1], taper_g)
            for c in c4:
                c.wait_recv()
            state = apply_mix(dmat, wbar, full_ref[...], cell_taper(0))
        else:
            state = apply_mix(dmat, wbar, state, cell_taper(1))
    res_ref[...] = state
    c5 = [
        remote(
            res_ref.at[rows((my + d) % NY)], out_ref.at[:, cols(my)],
            s5s.at[d - 1], s5r.at[d - 1], y_peer(d),
        )
        for d in range(1, NY)
    ]
    for c in c5:
        c.start()
    out_ref[:, cols(my)] = res_ref[rows(my), :]
    for c in c5:
        c.wait_recv()
    for c in c1 + c2 + c3[0] + c3[1] + c4 + c5:
        c.wait_send()


def local(ensemble, gauge_owner, gauge_block, gauge_weight, gauge_value, gauge_error, loc_level):
    members, cells = ensemble.shape
    gauges = gauge_block.shape[1]
    vmem = pl.BlockSpec(memory_space=pltpu.VMEM)
    dma = pltpu.SemaphoreType.DMA
    total = members * NY
    return pl.pallas_call(
        kernel,
        out_shape=jax.ShapeDtypeStruct((members, cells), F32),
        in_specs=[vmem] * 6 + [pl.BlockSpec(memory_space=pltpu.SMEM)],
        out_specs=vmem,
        scratch_shapes=[
            pltpu.VMEM((NBATCH * CAP, 128), F32),
            pltpu.VMEM((NBATCH * CAP, 128), F32),
            pltpu.VMEM((NBATCH * CAP * members, 128), F32),
            pltpu.VMEM((8, 128), F32),
            pltpu.VMEM((NZ, 8, 128), F32),
            pltpu.VMEM((NXC, NZ, 8, 128), F32),
            pltpu.VMEM((NBATCH, total, gauges), F32),
            pltpu.VMEM((total, cells // NY), F32),
            pltpu.VMEM((total, cells // NY), F32),
            pltpu.VMEM((total, total), F32),
            dma((7,)), dma((7,)), dma((7,)), dma((7,)), dma((NBATCH, 7)), dma((NBATCH, 7)),
            dma((7,)), dma((7,)), dma((7,)), dma((7,)),
        ],
        compiler_params=pltpu.CompilerParams(
            collective_id=0, has_side_effects=True, vmem_limit_bytes=48 * 2**20
        ),
    )(
        ensemble, gauge_owner.reshape(NBATCH, gauges), gauge_block, gauge_weight, gauge_value,
        gauge_error, loc_level,
    )


def solution(mesh):
    placed = (P("grp", "cells"), P(), P(), P(), P(), P(), P(None, "cells"))
    return jax.shard_map(
        local, mesh=mesh, in_specs=placed, out_specs=P("grp", "cells"), check_vma=False
    )
```

time: 521 us -> 74.4 us (0.14)
  the two profiles are of different devices: /device:TPU:1 before, /device:TPU:64 now
where the time goes in v1:
time: 74.4 us; the launch traced here: 74.2 us
  Pallas kernels  69.4 us (93%)
  local copies, waits for them, and re-layouts  4.78 us (6%)
    pallas_call x1, Pallas kernels, local(): pl.pallas_call(kernel, out_shape=jax.ShapeDtypeStruct((members, cells), F...  69.4 us
    unnamed x14, local copies, waits for them, and re-layouts  4.78 us

profile of v1, /device:TPU:64, one launch (start us, length us, event | category | flops | bytes accessed | tf_op | source)
XLA Modules:
  0.0 74.2 jit_solution(11535574968287386346)
XLA Ops:
  0.0 0.0 copy-start.3
  0.0 0.0 copy-start.2
  0.0 0.7 copy.10
  0.7 0.0 copy-start.5
  0.7 0.0 copy-done.3
  0.7 0.0 copy-done.2
  0.7 0.7 copy-done.5
  1.4 0.0 copy-start
  1.4 1.0 %copy-done = f32[2,512,128]{2,1,0:T(8,128)S(1)} copy-done((f32[2,512,128]{2,1,0:T(8,128)S(1)}, f32[2,512,128]{2,1,0:T(8,128)}, u32[]{:S(2)}) %copy-start) | copy-done | bytes 524312
  2.4 0.0 copy-start.1
  2.4 0.9 %copy-done.1 = f32[16,4096]{1,0:T(8,128)S(1)} copy-done((f32[16,4096]{1,0:T(8,128)S(1)}, f32[16,4096]{1,0:T(8,128)}, u32[]{:S(2)}) %copy-start.1) | copy-done | bytes 262168
  3.4 0.0 copy-start.4
  3.4 0.7 copy-done.4
  4.1 69.4 %shard_map.73 = f32[16,4096]{1,0:T(8,128)S(1)} custom-call(f32[16,4096]{1,0:T(8,128)S(1)} %copy-done.1, s32[2,512]{1,0:T(2,128)S(1)} %bitcast.3, s32[2,512]{1,0:T(2,128)S(1)} %copy-done.2, f32[2,512,128]{2,1,0:T(8,128)S(1)} %copy-done, f32[2,512]{1,0:T(2,128)S(1)} %copy-done.3, f32[2,512]{1,0:T(2,128)S(1)} %copy-done.4, s32[2,32]{1,0:T(2,128)S(1)} %copy-done.5), custom_call_target="tpu_custom_call" | custom-call | tf_op jit(solution)/shard_map/pallas_call | solution.py:354
  73.4 0.7 copy.12
Async XLA Ops:
  0.0 0.7 copy-start.3
  0.0 0.7 copy-start.2
  0.7 0.7 copy-start.5
  1.4 1.0 %copy-start = (f32[2,512,128]{2,1,0:T(8,128)S(1)}, f32[2,512,128]{2,1,0:T(8,128)}, u32[]{:S(2)}) copy-start(f32[2,512,128]{2,1,0:T(8,128)} %gw_ref.1) | copy-start | bytes 1572868
  2.4 0.9 %copy-start.1 = (f32[16,4096]{1,0:T(8,128)S(1)}, f32[16,4096]{1,0:T(8,128)}, u32[]{:S(2)}) copy-start(f32[16,4096]{1,0:T(8,128)} %ens_ref.1) | copy-start | bytes 786436
  3.4 0.7 copy-start.4

commit v2 on v1

v2 whole, which is shorter than its diff:
```python
import functools

import jax
import jax.numpy as jnp
from jax import lax
from jax.experimental import pallas as pl
from jax.experimental.pallas import tpu as pltpu
from jax.sharding import PartitionSpec as P

MESH = pl.DeviceIdType.MESH
F32, BF16, I32 = jnp.float32, jnp.bfloat16, jnp.int32
NBATCH = 2
NSIT = 12
CAP = 24
PIVOTS = 4
NX, NZ, NCORE = 4, 8, 2
NY = 8
NXC = NX * NCORE
FAR_FIRST = (4, 3, 5, 2, 6, 1, 7)


def split2(x):
    hi = x.astype(BF16)
    lo = (x - hi.astype(F32)).astype(BF16)
    return hi, lo


def split3(x):
    hi = x.astype(BF16)
    rest = x - hi.astype(F32)
    mid = rest.astype(BF16)
    lo = (rest - mid.astype(F32)).astype(BF16)
    return hi, mid, lo


def nn(a, b):
    return lax.dot_general(a, b, (((1,), (0,)), ((), ())), preferred_element_type=F32)


def nt(a, b):
    return lax.dot_general(a, b, (((1,), (1,)), ((), ())), preferred_element_type=F32)


def iota(shape, dim):
    return lax.broadcasted_iota(I32, shape, dim)


def wide(a, x):
    ah, al = split2(a)
    xh, xl = split2(x)
    left = jnp.concatenate([ah, al], axis=1)
    return nn(left, jnp.concatenate([xh, xh], axis=0)) + nn(ah, xl)


def ranks(o_row):
    count = o_row.shape[1]
    o_col = jnp.transpose(jnp.broadcast_to(o_row, (128, count)))
    tiles = []
    for t in range(count // 128):
        same = o_col == o_row[:, t * 128 : (t + 1) * 128]
        earlier = iota((count, 128), 0) > iota((count, 128), 1) + t * 128
        tiles.append(jnp.where(same & earlier, 1.0, 0.0).astype(BF16))
    equal = jnp.concatenate(tiles, axis=1)
    rank_col = nn(equal, jnp.ones((count, 128), BF16))
    rank_row = nt(jnp.ones((8, count), BF16), equal)[0:1]
    return o_col, rank_col, rank_row


def places(o_col, rank_col):
    o = o_col.astype(I32)
    r = rank_col.astype(I32)
    tile = ((o >> 4) * NCORE + (o & 1)) * NZ + ((o >> 1) & (NZ - 1))
    return (r >> 3) * (NXC * NZ) + tile, r & 7


def compact(grid3, row, group, members):
    count = row.shape[0]
    lanes = iota((count, 128), 1)
    onehot = jnp.concatenate(
        [
            jnp.where(row == lanes + t * 128, 1.0, 0.0).astype(BF16)
            for t in range(pl.cdiv(grid3.shape[0], 128))
        ],
        axis=1,
    )[:, : grid3.shape[0]]
    picked = nn(onehot, grid3)
    keep = (lanes >> 4) == group
    kept = jnp.concatenate(
        [jnp.where(keep, picked[:, t * 128 : (t + 1) * 128], 0.0).astype(BF16) for t in range(3)],
        axis=1,
    )
    fold = jnp.where((iota((members, 384), 1) & 15) == iota((members, 384), 0), 1.0, 0.0)
    return nt(fold.astype(BF16), kept)


def gauge_taper(levels, o_row, b_row):
    count = o_row.shape[1]
    i = iota((NXC * NZ, count), 0)
    xc, z = i >> 3, i & (NZ - 1)
    owner = ((xc >> 1) * NZ + z) * NCORE + (xc & 1)
    onehot = jnp.where(owner == o_row, 1.0, 0.0).astype(BF16)
    by_block = nn(jnp.transpose(levels).astype(BF16), onehot)
    hit = iota(by_block.shape, 0) == b_row
    return jnp.sum(jnp.where(hit, by_block, 0.0), axis=0, keepdims=True)


def innovations(prior, value, error):
    members = prior.shape[0]
    ymean = jnp.sum(prior, axis=0, keepdims=True) / members
    smat = (prior - ymean) * (1.0 / (error * jnp.sqrt(jnp.float32(members - 1))))
    dvec = (value - ymean) / error
    sh, sl = split2(smat)
    both = jnp.concatenate([sh, sl], axis=0)
    top = nt(sh, both)
    low = nt(sl, both)
    gram = top[:, :members] + (top[:, members:] + low[:, :members]) + low[:, members:]
    bvec = jnp.sum(smat * dvec, axis=1, keepdims=True)
    return gram, bvec


def stacked(x):
    hi, lo = split2(x)
    row = jnp.concatenate([hi, lo], axis=1)
    return jnp.concatenate([row, row], axis=0)


def halves(x):
    return jnp.concatenate(split2(x), axis=1)


def joined(x):
    n = x.shape[1] // 2
    return x[:, :n] + x[:, n:]


def newton(eye, y, z):
    wy, wz = stacked(y), stacked(z)
    q = 1.5 * eye - 0.5 * joined(nn(halves(z), wy))
    hq = halves(q)
    return joined(nn(hq, wy)), joined(nn(hq, wz))


def sweep(m_ref, j):
    n = m_ref.shape[0]
    span = range(PIVOTS)
    lane = iota((1, n), 1)
    m = m_ref[...]
    rows = [m_ref[pl.ds(j + i, 1), :] for i in span]
    at = [lane == j + i for i in span]
    e = [[None] * PIVOTS for _ in span]
    for i in span:
        for k in range(i, PIVOTS):
            e[i][k] = e[k][i] = jnp.sum(jnp.where(at[k], rows[i], 0.0), axis=1, keepdims=True)
    cols = [jnp.sum(jnp.where(at[k], m, 0.0), axis=1, keepdims=True) for k in span]
    for q in span:
        inv = 1.0 / e[q][q]
        scaled = [e[q][k] * inv for k in span]
        new = [[None] * PIVOTS for _ in span]
        for i in span:
            for k in range(i, PIVOTS):
                if i == q and k == q:
                    v = -inv
                elif i == q or k == q:
                    v = scaled[k if i == q else i]
                else:
                    v = e[i][k] - e[i][q] * scaled[k]
                new[i][k] = new[k][i] = v
        e = new
    u = []
    for i in span:
        acc = -e[i][0] * rows[0]
        for k in range(1, PIVOTS):
            acc = acc - e[i][k] * rows[k]
        for k in span:
            acc = jnp.where(at[k], e[i][k], acc)
        u.append(acc)
    pivot = functools.reduce(jnp.logical_or, at)
    new = jnp.where(pivot, 0.0, m)
    for i in span:
        new = new - cols[i] * u[i]
    m_ref[...] = new
    for i in span:
        m_ref[pl.ds(j + i, 1), :] = u[i]


def transform(m_ref, amat, eye, between):
    scal = jnp.sum(jnp.sum(amat * eye, axis=1, keepdims=True), axis=0, keepdims=True)
    m_ref[...] = amat
    steps = amat.shape[0] // PIVOTS
    most = NSIT - 2

    def three(i, carry):
        for k in range(3):
            sweep(m_ref, (i * 3 + k) * PIVOTS)
        return newton(eye, *carry)

    def one(i, carry):
        sweep(m_ref, (steps - NSIT + i) * PIVOTS)
        return newton(eye, *carry)

    carry = lax.fori_loop(0, most, three, (amat / scal, eye))
    between()
    _, z = lax.fori_loop(most, NSIT, one, carry)
    return z * lax.rsqrt(scal)


def apply_mix(dmat, wbar, x, taper):
    members = x.shape[0]
    anomaly = x - jnp.sum(x, axis=0, keepdims=True) / members
    shift = jnp.sum(wbar * anomaly, axis=0, keepdims=True) / jnp.sqrt(jnp.float32(members - 1))
    return x + taper * (wide(dmat, anomaly) + shift)


def kernel(
    ens_hbm, own_hbm, blk_hbm, gw_hbm, val_hbm, err_hbm, lvl_hbm, out_ref,
    ens_ref, own_ref, blk_ref, gw_ref, val_ref, err_ref, lvl_ref, cps,
    w_ref, b_ref, y_ref, row_ref, group_ref, tile_ref, line_ref, grid_ref, prior_ref, full_ref,
    res_ref, m_ref, s1s, s1r, s2s, s2r, s3s, s3r, s4s, s4r, s5s, s5r, s6s, s6r,
):
    members = ens_ref.shape[0]
    gauges = blk_ref.shape[1]
    half = gauges // NCORE
    cell = lax.axis_index("cells")
    my = lax.axis_index("grp")
    core = cell % NCORE
    mz = (cell // NCORE) % NZ
    mx = cell // (NCORE * NZ)
    mxc = mx * NCORE + core

    def z_peer(d):
        return ((mx * NZ + (mz + d) % NZ) * NCORE + core, my)

    def xc_peer(d):
        xc = (mxc + d) % NXC
        return (((xc // NCORE) * NZ + mz) * NCORE + xc % NCORE, my)

    def y_peer(d):
        return (cell, (my + d) % NY)

    twin = (cell + 1 - 2 * core, my)

    barrier = pltpu.get_barrier_semaphore()
    for d in FAR_FIRST:
        for peer in (z_peer(d), xc_peer(d), y_peer(d)):
            pl.semaphore_signal(barrier, inc=1, device_id=peer, device_id_type=MESH)

    pairs = [
        (own_hbm, own_ref), (blk_hbm, blk_ref), (gw_hbm, gw_ref), (lvl_hbm, lvl_ref),
        (ens_hbm, ens_ref), (val_hbm, val_ref), (err_hbm, err_ref),
    ]
    staged = [pltpu.make_async_copy(a, b, cps.at[i]) for i, (a, b) in enumerate(pairs)]
    for c in staged:
        c.start()
    for c in staged[:3]:
        c.wait()

    slot = iota((CAP, gauges), 0)
    for b in range(NBATCH):
        o_row = own_ref[b]
        o_col, rank_col, rank_row = ranks(o_row.astype(F32))
        row_ref[b], group_ref[b] = places(o_col, rank_col)
        mine = (o_row == cell) & (rank_row.astype(I32) == slot)
        pick = jnp.where(mine, 1.0, 0.0).astype(BF16)
        g0, g1, g2 = split3(gw_ref[b])
        w_ref[b * CAP : (b + 1) * CAP, :] = nn(pick, g0) + nn(pick, g1) + nn(pick, g2)
        blocks = jnp.broadcast_to(blk_ref[b : b + 1, :], (128, gauges)).astype(F32).astype(BF16)
        b_ref[b * CAP : (b + 1) * CAP, :] = nt(pick, blocks)

    for c in staged[3:]:
        c.wait()
    nblk = ens_ref.shape[1] // 128

    def reading(s, carry):
        want = b_ref[pl.ds(s, 1), :]
        got = jnp.zeros((members, 128), F32)
        for k in range(nblk):
            got = jnp.where(want == k, ens_ref[:, k * 128 : (k + 1) * 128], got)
        y_ref[pl.ds(pl.multiple_of(s * members, members), members), :] = got * w_ref[pl.ds(s, 1), :]
        return carry

    lax.fori_loop(0, NBATCH * CAP, reading, 0)
    y3 = jnp.concatenate(split3(y_ref[...]), axis=1)
    flat = nt(jnp.ones((8, y3.shape[1]), BF16), y3)[:4]
    sub = iota((4, 128), 0)
    lane = iota((4, 128), 1)
    for b in range(NBATCH):
        tile = jnp.zeros((4, 128), F32)
        for r in range(3):
            tile = jnp.where(sub == r, flat[:, (3 * b + r) * 128 : (3 * b + r + 1) * 128], tile)
        if b == 0:
            for k in range(nblk):
                level = lvl_ref[0, k].astype(F32) * 0.25
                tile = jnp.where((sub == 3) & (lane == k), level, tile)
        tile_ref[b] = tile

    pl.semaphore_wait(barrier, 21)

    def remote(src, dst, send, recv, peer):
        return pltpu.make_async_remote_copy(
            src_ref=src, dst_ref=dst, send_sem=send, recv_sem=recv,
            device_id=peer, device_id_type=MESH,
        )

    chunk = ens_ref.shape[1] // NY

    def rows(y):
        return pl.ds(pl.multiple_of(y * members, members), members)

    def cols(y):
        return pl.ds(pl.multiple_of(y * chunk, chunk), chunk)

    c1 = [
        remote(tile_ref, line_ref.at[:, mz], s1s.at[d - 1], s1r.at[d - 1], z_peer(d))
        for d in FAR_FIRST
    ]
    for c in c1:
        c.start()
    for b in range(NBATCH):
        line_ref[b, mz] = tile_ref[b]
    c4 = [
        remote(
            ens_ref.at[:, cols((my + d) % NY)], full_ref.at[rows(my)],
            s4s.at[d - 1], s4r.at[d - 1], y_peer(d),
        )
        for d in FAR_FIRST
    ]
    for c in c4:
        c.start()
    full_ref[rows(my), :] = ens_ref[:, cols(my)]
    for c in c1:
        c.wait_recv()
    c2 = [
        [
            remote(
                line_ref.at[b], grid_ref.at[b, mxc], s2s.at[b, d - 1], s2r.at[b, d - 1], xc_peer(d)
            )
            for d in FAR_FIRST
        ]
        for b in range(NBATCH)
    ]
    c3 = [
        [
            remote(
                prior_ref.at[b, core, rows(my)], prior_ref.at[b, core, rows(my)],
                s3s.at[b, d - 1], s3r.at[b, d - 1], y_peer(d),
            )
            for d in FAR_FIRST
        ]
        for b in range(NBATCH)
    ]
    c6 = [
        [
            remote(
                prior_ref.at[b, core, rows((my + NY - d) % NY)],
                prior_ref.at[b, core, rows((my + NY - d) % NY)],
                s6s.at[b, d], s6r.at[b, d], twin,
            )
            for d in (0,) + FAR_FIRST
        ]
        for b in range(NBATCH)
    ]

    def packed(b):
        parts = [grid_ref[b, :, :, r, :].reshape(NXC * NZ, 128) for r in range(3)]
        grid3 = jnp.concatenate(split3(jnp.concatenate(parts, axis=0)), axis=1)
        mine = pl.ds(pl.multiple_of(core * half, half), half)
        prior_ref[b, core, rows(my), :] = compact(
            grid3, row_ref[b, mine, :], group_ref[b, mine, :], members
        )

    def onward(b):
        for c, f in zip(c3[b][::-1], c6[b][:0:-1]):
            c.wait_recv()
            f.start()

    for b in range(NBATCH):
        for c in c2[b]:
            c.start()
        grid_ref[b, mxc] = line_ref[b]
    for c in c2[0]:
        c.wait_recv()
    packed(0)
    for c in c3[0] + c6[0][:1]:
        c.start()
    for c in c2[1]:
        c.wait_recv()
    packed(1)
    levels = grid_ref[0, :, :, 3, :].reshape(NXC * NZ, 128)
    taper_g = gauge_taper(levels, own_ref[1], blk_ref[1:2, :])
    onward(0)
    for c in c3[1] + c6[1][:1]:
        c.start()
    for c in c6[0]:
        c.wait_recv()

    def cell_taper(b):
        each = [
            jnp.full((1, 128), lvl_ref[b, my * (chunk // 128) + k].astype(F32) * 0.25, F32)
            for k in range(chunk // 128)
        ]
        return jnp.concatenate(each, axis=1)

    def prior_of(b):
        return jnp.concatenate([prior_ref[b, h] for h in range(NCORE)], axis=1)

    total = members * NY
    eye = jnp.where(iota((total, total), 0) == iota((total, total), 1), 1.0, 0.0)
    prior = prior_of(0)
    for b in range(NBATCH):
        gram, bvec = innovations(prior, val_ref[b : b + 1, :], err_ref[b : b + 1, :])
        amat = eye + gram
        between = functools.partial(onward, 1) if b == 0 else lambda: None
        dmat = transform(m_ref, amat, eye, between) - eye
        b_row = jnp.sum(eye * bvec, axis=0, keepdims=True)
        wbar = -jnp.sum(m_ref[...] * b_row, axis=1, keepdims=True)
        if b == 0:
            for c in c6[1]:
                c.wait_recv()
            prior = apply_mix(dmat, wbar, prior_of(1), taper_g)
            for c in c4:
                c.wait_recv()
            state = apply_mix(dmat, wbar, full_ref[...], cell_taper(0))
        else:
            state = apply_mix(dmat, wbar, state, cell_taper(1))
    res_ref[...] = state
    c5 = [
        remote(
            res_ref.at[rows((my + d) % NY)], out_ref.at[:, cols(my)],
            s5s.at[d - 1], s5r.at[d - 1], y_peer(d),
        )
        for d in FAR_FIRST
    ]
    for c in c5:
        c.start()
    out_ref[:, cols(my)] = res_ref[rows(my), :]
    for c in c5:
        c.wait_recv()
    for c in c1 + c2[0] + c2[1] + c3[0] + c3[1] + c4 + c5 + c6[0] + c6[1]:
        c.wait_send()


def local(ensemble, gauge_owner, gauge_block, gauge_weight, gauge_value, gauge_error, loc_level):
    members, cells = ensemble.shape
    gauges = gauge_block.shape[1]
    vmem = pl.BlockSpec(memory_space=pltpu.VMEM)
    hbm = pl.BlockSpec(memory_space=pltpu.HBM)
    dma = pltpu.SemaphoreType.DMA
    total = members * NY
    operands = (
        ensemble, jnp.swapaxes(gauge_owner, 1, 2), gauge_block, gauge_weight, gauge_value,
        gauge_error, loc_level,
    )
    staged = [pltpu.VMEM(a.shape, a.dtype) for a in operands[:-1]]
    return pl.pallas_call(
        kernel,
        out_shape=jax.ShapeDtypeStruct((members, cells), F32),
        in_specs=[hbm] * 7,
        out_specs=vmem,
        scratch_shapes=staged + [
            pltpu.SMEM(loc_level.shape, I32),
            dma((7,)),
            pltpu.VMEM((NBATCH * CAP, 128), F32),
            pltpu.VMEM((NBATCH * CAP, 128), F32),
            pltpu.VMEM((NBATCH * CAP * members, 128), F32),
            pltpu.VMEM((NBATCH, gauges, 128), I32),
            pltpu.VMEM((NBATCH, gauges, 128), I32),
            pltpu.VMEM((NBATCH, 4, 128), F32),
            pltpu.VMEM((NBATCH, NZ, 4, 128), F32),
            pltpu.VMEM((NBATCH, NXC, NZ, 4, 128), F32),
            pltpu.VMEM((NBATCH, NCORE, total, gauges // NCORE), F32),
            pltpu.VMEM((total, cells // NY), F32),
            pltpu.VMEM((total, cells // NY), F32),
            pltpu.VMEM((total, total), F32),
            dma((7,)), dma((7,)), dma((NBATCH, 7)), dma((NBATCH, 7)), dma((NBATCH, 7)),
            dma((NBATCH, 7)), dma((7,)), dma((7,)), dma((7,)), dma((7,)),
            dma((NBATCH, 8)), dma((NBATCH, 8)),
        ],
        compiler_params=pltpu.CompilerParams(
            collective_id=0, has_side_effects=True, vmem_limit_bytes=63 * 2**20
        ),
    )(*operands)


def solution(mesh):
    placed = (P("grp", "cells"), P(), P(), P(), P(), P(), P(None, "cells"))
    return jax.shard_map(
        local, mesh=mesh, in_specs=placed, out_specs=P("grp", "cells"), check_vma=False
    )
```

time: 74.4 us -> 56.2 us (0.76)
  the two profiles are of different devices: /device:TPU:64 before, /device:TPU:1 now
where the time goes in v2:
time: 56.2 us; the launch traced here: 56.1 us
  Pallas kernels  54.4 us (97%)
  local copies, waits for them, and re-layouts  1.67 us (3%)
    pallas_call x1, Pallas kernels, local(): pl.pallas_call(kernel, out_shape=jax.ShapeDtypeStruct((members, cells), F...  54.4 us
    unnamed x1, local copies, waits for them, and re-layouts  1.67 us

profile of v2, /device:TPU:1, one launch (start us, length us, event | category | flops | bytes accessed | tf_op | source)
XLA Modules:
  0.0 56.1 jit_solution(6102296538367432565)
XLA Ops:
  0.0 54.4 %shard_map.73 = f32[16,4096]{1,0:T(8,128)} custom-call(f32[16,4096]{1,0:T(8,128)} %ens_hbm.1, s32[2,1,512]{2,1,0:T(1,128)} %bitcast.1, s32[2,512]{1,0:T(2,128)} %blk_hbm.1, f32[2,512,128]{2,1,0:T(8,128)} %gw_hbm.1, f32[2,512]{1,0:T(2,128)} %val_hbm.1, f32[2,512]{1,0:T(2,128)} %err_hbm.1, s32[2,32]{1,0:T(2,128)} %lvl_hbm.1), custom_call_target="tpu_custom_call" | custom-call | tf_op jit(solution)/shard_map/pallas_call | solution.py:454
  54.4 1.7 %copy.9 = f32[16,4096]{1,0:T(8,128)} copy(f32[16,4096]{1,0:T(8,128)} %shard_map.73) | data formatting | bytes 524288

commit v3 on v2

--- a/solution.py
+++ b/solution.py
@@ -245,53 +245,56 @@
             pl.semaphore_signal(barrier, inc=1, device_id=peer, device_id_type=MESH)
 
     pairs = [
-        (own_hbm, own_ref), (blk_hbm, blk_ref), (gw_hbm, gw_ref), (lvl_hbm, lvl_ref),
-        (ens_hbm, ens_ref), (val_hbm, val_ref), (err_hbm, err_ref),
+        (own_hbm, own_ref), (blk_hbm, blk_ref), (gw_hbm.at[0], gw_ref.at[0]), (ens_hbm, ens_ref),
+        (lvl_hbm, lvl_ref), (gw_hbm.at[1], gw_ref.at[1]), (val_hbm, val_ref), (err_hbm, err_ref),
     ]
     staged = [pltpu.make_async_copy(a, b, cps.at[i]) for i, (a, b) in enumerate(pairs)]
     for c in staged:
         c.start()
-    for c in staged[:3]:
-        c.wait()
-
-    slot = iota((CAP, gauges), 0)
-    for b in range(NBATCH):
+    nblk = ens_ref.shape[1] // 128
+
+    def readings(b):
+        slot = iota((CAP, gauges), 0)
         o_row = own_ref[b]
         o_col, rank_col, rank_row = ranks(o_row.astype(F32))
         row_ref[b], group_ref[b] = places(o_col, rank_col)
         mine = (o_row == cell) & (rank_row.astype(I32) == slot)
         pick = jnp.where(mine, 1.0, 0.0).astype(BF16)
         g0, g1, g2 = split3(gw_ref[b])
-        w_ref[b * CAP : (b + 1) * CAP, :] = nn(pick, g0) + nn(pick, g1) + nn(pick, g2)
+        w_ref[...] = nn(pick, g0) + nn(pick, g1) + nn(pick, g2)
         blocks = jnp.broadcast_to(blk_ref[b : b + 1, :], (128, gauges)).astype(F32).astype(BF16)
-        b_ref[b * CAP : (b + 1) * CAP, :] = nt(pick, blocks)
-
-    for c in staged[3:]:
-        c.wait()
-    nblk = ens_ref.shape[1] // 128
-
-    def reading(s, carry):
-        want = b_ref[pl.ds(s, 1), :]
-        got = jnp.zeros((members, 128), F32)
-        for k in range(nblk):
-            got = jnp.where(want == k, ens_ref[:, k * 128 : (k + 1) * 128], got)
-        y_ref[pl.ds(pl.multiple_of(s * members, members), members), :] = got * w_ref[pl.ds(s, 1), :]
-        return carry
-
-    lax.fori_loop(0, NBATCH * CAP, reading, 0)
-    y3 = jnp.concatenate(split3(y_ref[...]), axis=1)
-    flat = nt(jnp.ones((8, y3.shape[1]), BF16), y3)[:4]
-    sub = iota((4, 128), 0)
-    lane = iota((4, 128), 1)
-    for b in range(NBATCH):
+        b_ref[...] = nt(pick, blocks)
+        if b == 0:
+            staged[3].wait()
+
+        def reading(s, carry):
+            want = b_ref[pl.ds(s, 1), :]
+            got = jnp.zeros((members, 128), F32)
+            for k in range(nblk):
+                got = jnp.where(want == k, ens_ref[:, k * 128 : (k + 1) * 128], got)
+            at = pl.ds(pl.multiple_of(s * members, members), members)
+            y_ref[at, :] = got * w_ref[pl.ds(s, 1), :]
+            return carry
+
+        lax.fori_loop(0, CAP, reading, 0, unroll=4)
+        y3 = jnp.concatenate(split3(y_ref[...]), axis=1)
+        flat = nt(jnp.ones((8, y3.shape[1]), BF16), y3)[:4]
+        sub = iota((4, 128), 0)
+        lane = iota((4, 128), 1)
         tile = jnp.zeros((4, 128), F32)
         for r in range(3):
-            tile = jnp.where(sub == r, flat[:, (3 * b + r) * 128 : (3 * b + r + 1) * 128], tile)
-        if b == 0:
+            tile = jnp.where(sub == r, flat[:, r * 128 : (r + 1) * 128], tile)
+        if b == 1:
             for k in range(nblk):
                 level = lvl_ref[0, k].astype(F32) * 0.25
                 tile = jnp.where((sub == 3) & (lane == k), level, tile)
         tile_ref[b] = tile
+
+    for c in staged[:3]:
+        c.wait()
+    readings(0)
+    for c in staged[4:]:
+        c.wait()
 
     pl.semaphore_wait(barrier, 21)
 
@@ -310,13 +313,14 @@
         return pl.ds(pl.multiple_of(y * chunk, chunk), chunk)
 
     c1 = [
-        remote(tile_ref, line_ref.at[:, mz], s1s.at[d - 1], s1r.at[d - 1], z_peer(d))
-        for d in FAR_FIRST
-    ]
-    for c in c1:
-        c.start()
-    for b in range(NBATCH):
-        line_ref[b, mz] = tile_ref[b]
+        [
+            remote(
+                tile_ref.at[b], line_ref.at[b, mz], s1s.at[b, d - 1], s1r.at[b, d - 1], z_peer(d)
+            )
+            for d in FAR_FIRST
+        ]
+        for b in range(NBATCH)
+    ]
     c4 = [
         remote(
             ens_ref.at[:, cols((my + d) % NY)], full_ref.at[rows(my)],
@@ -324,11 +328,14 @@
         )
         for d in FAR_FIRST
     ]
-    for c in c4:
+    for c in c1[0] + c4:
+        c.start()
+    readings(1)
+    for c in c1[1]:
         c.start()
     full_ref[rows(my), :] = ens_ref[:, cols(my)]
-    for c in c1:
-        c.wait_recv()
+    for b in range(NBATCH):
+        line_ref[b, mz] = tile_ref[b]
     c2 = [
         [
             remote(
@@ -374,6 +381,8 @@
             f.start()
 
     for b in range(NBATCH):
+        for c in c1[b]:
+            c.wait_recv()
         for c in c2[b]:
             c.start()
         grid_ref[b, mxc] = line_ref[b]
@@ -385,12 +394,12 @@
     for c in c2[1]:
         c.wait_recv()
     packed(1)
-    levels = grid_ref[0, :, :, 3, :].reshape(NXC * NZ, 128)
+    levels = grid_ref[1, :, :, 3, :].reshape(NXC * NZ, 128)
     taper_g = gauge_taper(levels, own_ref[1], blk_ref[1:2, :])
     onward(0)
     for c in c3[1] + c6[1][:1]:
         c.start()
-    for c in c6[0]:
+    for c in c6[0] + c4:
         c.wait_recv()
 
     def cell_taper(b):
@@ -417,8 +426,6 @@
             for c in c6[1]:
                 c.wait_recv()
             prior = apply_mix(dmat, wbar, prior_of(1), taper_g)
-            for c in c4:
-                c.wait_recv()
             state = apply_mix(dmat, wbar, full_ref[...], cell_taper(0))
         else:
             state = apply_mix(dmat, wbar, state, cell_taper(1))
@@ -435,7 +442,7 @@
     out_ref[:, cols(my)] = res_ref[rows(my), :]
     for c in c5:
         c.wait_recv()
-    for c in c1 + c2[0] + c2[1] + c3[0] + c3[1] + c4 + c5 + c6[0] + c6[1]:
+    for c in c1[0] + c1[1] + c2[0] + c2[1] + c3[0] + c3[1] + c4 + c5 + c6[0] + c6[1]:
         c.wait_send()
 
 
@@ -453,15 +460,15 @@
     staged = [pltpu.VMEM(a.shape, a.dtype) for a in operands[:-1]]
     return pl.pallas_call(
         kernel,
-        out_shape=jax.ShapeDtypeStruct((members, cells), F32),
+        out_shape=pltpu.VMEM((members, cells), F32),
         in_specs=[hbm] * 7,
         out_specs=vmem,
         scratch_shapes=staged + [
             pltpu.SMEM(loc_level.shape, I32),
-            dma((7,)),
-            pltpu.VMEM((NBATCH * CAP, 128), F32),
-            pltpu.VMEM((NBATCH * CAP, 128), F32),
-            pltpu.VMEM((NBATCH * CAP * members, 128), F32),
+            dma((8,)),
+            pltpu.VMEM((CAP, 128), F32),
+            pltpu.VMEM((CAP, 128), F32),
+            pltpu.VMEM((CAP * members, 128), F32),
             pltpu.VMEM((NBATCH, gauges, 128), I32),
             pltpu.VMEM((NBATCH, gauges, 128), I32),
             pltpu.VMEM((NBATCH, 4, 128), F32),
@@ -471,12 +478,12 @@
             pltpu.VMEM((total, cells // NY), F32),
             pltpu.VMEM((total, cells // NY), F32),
             pltpu.VMEM((total, total), F32),
-            dma((7,)), dma((7,)), dma((NBATCH, 7)), dma((NBATCH, 7)), dma((NBATCH, 7)),
-            dma((NBATCH, 7)), dma((7,)), dma((7,)), dma((7,)), dma((7,)),
+            dma((NBATCH, 7)), dma((NBATCH, 7)), dma((NBATCH, 7)), dma((NBATCH, 7)),
+            dma((NBATCH, 7)), dma((NBATCH, 7)), dma((7,)), dma((7,)), dma((7,)), dma((7,)),
             dma((NBATCH, 8)), dma((NBATCH, 8)),
         ],
         compiler_params=pltpu.CompilerParams(
-            collective_id=0, has_side_effects=True, vmem_limit_bytes=63 * 2**20
+            collective_id=0, has_side_effects=True, vmem_limit_bytes=60 * 2**20
         ),
     )(*operands)
 

time: 56.2 us -> 53.1 us (0.945)
  Pallas kernels: 54.4 us -> 52.2 us
  local copies, waits for them, and re-layouts: 1.67 us -> 0.71 us
    pallas_call x1, Pallas kernels: 54.4 us -> 52.2 us  [local(): pl.pallas_call(kernel, out_shape=pltpu.VMEM((members, cells), F32), in_sp...]
    unnamed x1, local copies, waits for them, and re-layouts: 1.67 us -> 0.71 us
where the time goes in v3:
time: 53.1 us; the launch traced here: 53 us
  Pallas kernels  52.2 us (98%)
  local copies, waits for them, and re-layouts  0.71 us (1%)
    pallas_call x1, Pallas kernels, local(): pl.pallas_call(kernel, out_shape=pltpu.VMEM((members, cells), F32), in_sp...  52.2 us

profile of v3, /device:TPU:1, one launch (start us, length us, event | category | flops | bytes accessed | tf_op | source)
XLA Modules:
  0.0 53.0 jit_solution(16969163009658273134)
XLA Ops:
  0.0 52.2 %shard_map.73 = f32[16,4096]{1,0:T(8,128)S(1)} custom-call(f32[16,4096]{1,0:T(8,128)} %ens_hbm.1, s32[2,1,512]{2,1,0:T(1,128)} %bitcast.1, s32[2,512]{1,0:T(2,128)} %blk_hbm.1, f32[2,512,128]{2,1,0:T(8,128)} %gw_hbm.1, f32[2,512]{1,0:T(2,128)} %val_hbm.1, f32[2,512]{1,0:T(2,128)} %err_hbm.1, s32[2,32]{1,0:T(2,128)} %lvl_hbm.1), custom_call_target="tpu_custom_call" | custom-call | tf_op jit(solution)/shard_map/pallas_call | solution.py:461
  52.3 0.7 %copy.9 = f32[16,4096]{1,0:T(8,128)} copy(f32[16,4096]{1,0:T(8,128)S(1)} %shard_map.73) | data formatting | bytes 524288

commit v4 on v3

--- a/solution.py
+++ b/solution.py
@@ -17,6 +17,7 @@
 NY = 8
 NXC = NX * NCORE
 FAR_FIRST = (4, 3, 5, 2, 6, 1, 7)
+NEAR = (6, 5, 4, 3, 2, 1, 0)
 
 
 def split2(x):
@@ -183,7 +184,7 @@
         m_ref[pl.ds(j + i, 1), :] = u[i]
 
 
-def transform(m_ref, amat, eye, between):
+def transform(m_ref, amat, eye, stops):
     scal = jnp.sum(jnp.sum(amat * eye, axis=1, keepdims=True), axis=0, keepdims=True)
     m_ref[...] = amat
     steps = amat.shape[0] // PIVOTS
@@ -198,24 +199,26 @@
         sweep(m_ref, (steps - NSIT + i) * PIVOTS)
         return newton(eye, *carry)
 
-    carry = lax.fori_loop(0, most, three, (amat / scal, eye))
-    between()
+    carry, done = (amat / scal, eye), 0
+    for stop, act in stops:
+        carry = lax.fori_loop(done, stop, three, carry)
+        act()
+        done = stop
+    carry = lax.fori_loop(done, most, three, carry)
     _, z = lax.fori_loop(most, NSIT, one, carry)
     return z * lax.rsqrt(scal)
 
 
-def apply_mix(dmat, wbar, x, taper):
-    members = x.shape[0]
-    anomaly = x - jnp.sum(x, axis=0, keepdims=True) / members
-    shift = jnp.sum(wbar * anomaly, axis=0, keepdims=True) / jnp.sqrt(jnp.float32(members - 1))
-    return x + taper * (wide(dmat, anomaly) + shift)
+def apply_mix(mixer, x, taper):
+    anomaly = x - jnp.sum(x, axis=0, keepdims=True) / x.shape[0]
+    return x + taper * wide(mixer, anomaly)
 
 
 def kernel(
     ens_hbm, own_hbm, blk_hbm, gw_hbm, val_hbm, err_hbm, lvl_hbm, out_ref,
     ens_ref, own_ref, blk_ref, gw_ref, val_ref, err_ref, lvl_ref, cps,
     w_ref, b_ref, y_ref, row_ref, group_ref, tile_ref, line_ref, grid_ref, prior_ref, full_ref,
-    res_ref, m_ref, s1s, s1r, s2s, s2r, s3s, s3r, s4s, s4r, s5s, s5r, s6s, s6r,
+    mix_ref, taper_ref, m_ref, s1s, s1r, s2s, s2r, s3s, s3r, s4s, s4r, s6s, s6r,
 ):
     members = ens_ref.shape[0]
     gauges = blk_ref.shape[1]
@@ -247,6 +250,7 @@
     pairs = [
         (own_hbm, own_ref), (blk_hbm, blk_ref), (gw_hbm.at[0], gw_ref.at[0]), (ens_hbm, ens_ref),
         (lvl_hbm, lvl_ref), (gw_hbm.at[1], gw_ref.at[1]), (val_hbm, val_ref), (err_hbm, err_ref),
+        (ens_hbm, full_ref.at[pl.ds(pl.multiple_of(my * members, members), members)]),
     ]
     staged = [pltpu.make_async_copy(a, b, cps.at[i]) for i, (a, b) in enumerate(pairs)]
     for c in staged:
@@ -304,13 +308,32 @@
             device_id=peer, device_id_type=MESH,
         )
 
-    chunk = ens_ref.shape[1] // NY
+    chunk = ens_ref.shape[1] // 2
 
     def rows(y):
         return pl.ds(pl.multiple_of(y * members, members), members)
 
-    def cols(y):
-        return pl.ds(pl.multiple_of(y * chunk, chunk), chunk)
+    def ring(way, step, part):
+        block = rows((my + (step - 1) * (NY - way)) % NY)
+        half_block = pl.ds((part if way == 1 else 1 - part) * chunk, chunk)
+        at = (0 if way == 1 else 1, step - 1, part)
+        here = full_ref.at[block, half_block]
+        return remote(here, here, s4s.at[at], s4r.at[at], (cell, (my + way) % NY))
+
+    hops = {
+        (step, part): [ring(way, step, part) for way in (1, NY - 1)]
+        for step in range(1, NY // 2 + 1)
+        for part in range(1 if step == NY // 2 else 2)
+    }
+
+    def arrive(step, part):
+        for c in hops[step, part]:
+            c.wait_recv()
+
+    def forward(step, part):
+        arrive(step - 1, part)
+        for c in hops[step, part]:
+            c.start()
 
     c1 = [
         [
@@ -321,19 +344,11 @@
         ]
         for b in range(NBATCH)
     ]
-    c4 = [
-        remote(
-            ens_ref.at[:, cols((my + d) % NY)], full_ref.at[rows(my)],
-            s4s.at[d - 1], s4r.at[d - 1], y_peer(d),
-        )
-        for d in FAR_FIRST
-    ]
-    for c in c1[0] + c4:
+    for c in c1[0] + hops[1, 0]:
         c.start()
     readings(1)
-    for c in c1[1]:
+    for c in c1[1] + hops[1, 1]:
         c.start()
-    full_ref[rows(my), :] = ens_ref[:, cols(my)]
     for b in range(NBATCH):
         line_ref[b, mz] = tile_ref[b]
     c2 = [
@@ -375,10 +390,10 @@
             grid3, row_ref[b, mine, :], group_ref[b, mine, :], members
         )
 
-    def onward(b):
-        for c, f in zip(c3[b][::-1], c6[b][:0:-1]):
-            c.wait_recv()
-            f.start()
+    def onward(b, ranks):
+        for k in ranks:
+            c3[b][k].wait_recv()
+            c6[b][k + 1].start()
 
     for b in range(NBATCH):
         for c in c1[b]:
@@ -386,6 +401,7 @@
         for c in c2[b]:
             c.start()
         grid_ref[b, mxc] = line_ref[b]
+    forward(2, 0)
     for c in c2[0]:
         c.wait_recv()
     packed(0)
@@ -396,53 +412,69 @@
     packed(1)
     levels = grid_ref[1, :, :, 3, :].reshape(NXC * NZ, 128)
     taper_g = gauge_taper(levels, own_ref[1], blk_ref[1:2, :])
-    onward(0)
+    for b in range(NBATCH):
+        for k in range(nblk):
+            level = lvl_ref[b, k].astype(F32) * 0.25
+            taper_ref[b : b + 1, k * 128 : (k + 1) * 128] = jnp.full((1, 128), level, F32)
+    onward(0, NEAR[:4])
+    forward(2, 1)
+    onward(0, NEAR[4:])
     for c in c3[1] + c6[1][:1]:
         c.start()
-    for c in c6[0] + c4:
+    for c in c6[0]:
         c.wait_recv()
 
-    def cell_taper(b):
-        each = [
-            jnp.full((1, 128), lvl_ref[b, my * (chunk // 128) + k].astype(F32) * 0.25, F32)
-            for k in range(chunk // 128)
-        ]
-        return jnp.concatenate(each, axis=1)
+    def at_1_2():
+        forward(3, 0)
+
+    def at_1_7():
+        forward(3, 1)
+
+    def at_1_9():
+        onward(1, NEAR)
+
+    def at_2_2():
+        forward(4, 0)
+
+    stops = [[(2, at_1_2), (7, at_1_7), (9, at_1_9)], [(2, at_2_2)]]
 
     def prior_of(b):
         return jnp.concatenate([prior_ref[b, h] for h in range(NCORE)], axis=1)
 
     total = members * NY
     eye = jnp.where(iota((total, total), 0) == iota((total, total), 1), 1.0, 0.0)
+    scale = 1.0 / jnp.sqrt(jnp.float32(total - 1))
     prior = prior_of(0)
     for b in range(NBATCH):
         gram, bvec = innovations(prior, val_ref[b : b + 1, :], err_ref[b : b + 1, :])
         amat = eye + gram
-        between = functools.partial(onward, 1) if b == 0 else lambda: None
-        dmat = transform(m_ref, amat, eye, between) - eye
-        b_row = jnp.sum(eye * bvec, axis=0, keepdims=True)
-        wbar = -jnp.sum(m_ref[...] * b_row, axis=1, keepdims=True)
+        dmat = transform(m_ref, amat, eye, stops[b]) - eye
+        w_row = -jnp.sum(m_ref[...] * bvec, axis=0, keepdims=True)
+        mixer = dmat + w_row * scale
+        mix_ref[b] = mixer
         if b == 0:
             for c in c6[1]:
                 c.wait_recv()
-            prior = apply_mix(dmat, wbar, prior_of(1), taper_g)
-            state = apply_mix(dmat, wbar, full_ref[...], cell_taper(0))
-        else:
-            state = apply_mix(dmat, wbar, state, cell_taper(1))
-    res_ref[...] = state
-    c5 = [
-        remote(
-            res_ref.at[rows((my + d) % NY)], out_ref.at[:, cols(my)],
-            s5s.at[d - 1], s5r.at[d - 1], y_peer(d),
-        )
-        for d in FAR_FIRST
-    ]
-    for c in c5:
-        c.start()
-    out_ref[:, cols(my)] = res_ref[rows(my), :]
-    for c in c5:
-        c.wait_recv()
-    for c in c1[0] + c1[1] + c2[0] + c2[1] + c3[0] + c3[1] + c4 + c5 + c6[0] + c6[1]:
+            centred = mixer - jnp.sum(mixer, axis=0, keepdims=True) / total
+            prior = apply_mix(mixer, prior_of(1), taper_g)
+    own = [mix_ref[b, rows(my), :] for b in range(NBATCH)]
+    stack = jnp.concatenate(own + [wide(own[1], centred)], axis=0)
+    hi, lo = split2(stack)
+    left = jnp.concatenate([hi, lo], axis=1)
+    for step, part in hops:
+        if (step + 1, part) not in hops:
+            arrive(step, part)
+    width = 512
+    for i in range(ens_ref.shape[1] // width):
+        at = slice(i * width, (i + 1) * width)
+        x = full_ref[:, at]
+        xh, xl = split2(x - jnp.sum(x, axis=0, keepdims=True) / total)
+        both = nn(left, jnp.concatenate([xh, xh], axis=0)) + nn(hi, xl)
+        t0, t1 = taper_ref[0:1, at], taper_ref[1:2, at]
+        first, second, third = (both[k * members : (k + 1) * members] for k in range(3))
+        out_ref[:, at] = ens_ref[:, at] + t0 * first + t1 * (second + t0 * third)
+    sent = [c for group in hops.values() for c in group]
+    for c in c1[0] + c1[1] + c2[0] + c2[1] + c3[0] + c3[1] + c6[0] + c6[1] + sent:
         c.wait_send()
 
 
@@ -465,7 +497,7 @@
         out_specs=vmem,
         scratch_shapes=staged + [
             pltpu.SMEM(loc_level.shape, I32),
-            dma((8,)),
+            dma((9,)),
             pltpu.VMEM((CAP, 128), F32),
             pltpu.VMEM((CAP, 128), F32),
             pltpu.VMEM((CAP * members, 128), F32),
@@ -475,11 +507,12 @@
             pltpu.VMEM((NBATCH, NZ, 4, 128), F32),
             pltpu.VMEM((NBATCH, NXC, NZ, 4, 128), F32),
             pltpu.VMEM((NBATCH, NCORE, total, gauges // NCORE), F32),
-            pltpu.VMEM((total, cells // NY), F32),
-            pltpu.VMEM((total, cells // NY), F32),
+            pltpu.VMEM((total, cells), F32),
+            pltpu.VMEM((NBATCH, total, total), F32),
+            pltpu.VMEM((NBATCH, cells), F32),
             pltpu.VMEM((total, total), F32),
             dma((NBATCH, 7)), dma((NBATCH, 7)), dma((NBATCH, 7)), dma((NBATCH, 7)),
-            dma((NBATCH, 7)), dma((NBATCH, 7)), dma((7,)), dma((7,)), dma((7,)), dma((7,)),
+            dma((NBATCH, 7)), dma((NBATCH, 7)), dma((2, 4, 2)), dma((2, 4, 2)),
             dma((NBATCH, 8)), dma((NBATCH, 8)),
         ],
         compiler_params=pltpu.CompilerParams(

time: 53.1 us -> 49.2 us (0.927)
  Pallas kernels: 52.2 us -> 48.3 us
    pallas_call x1, Pallas kernels: 52.2 us -> 48.3 us  [local(): pl.pallas_call(kernel, out_shape=pltpu.VMEM((members, cells), F32), in_sp...]
where the time goes in v4:
time: 49.2 us; the launch traced here: 49.1 us
  Pallas kernels  48.3 us (98%)
  local copies, waits for them, and re-layouts  0.71 us (1%)
    pallas_call x1, Pallas kernels, local(): pl.pallas_call(kernel, out_shape=pltpu.VMEM((members, cells), F32), in_sp...  48.3 us

profile of v4, /device:TPU:1, one launch (start us, length us, event | category | flops | bytes accessed | tf_op | source)
XLA Modules:
  0.0 49.1 jit_solution(10336138714515123623)
XLA Ops:
  0.0 48.3 %shard_map.73 = f32[16,4096]{1,0:T(8,128)S(1)} custom-call(f32[16,4096]{1,0:T(8,128)} %ens_hbm.1, s32[2,1,512]{2,1,0:T(1,128)} %bitcast.1, s32[2,512]{1,0:T(2,128)} %blk_hbm.1, f32[2,512,128]{2,1,0:T(8,128)} %gw_hbm.1, f32[2,512]{1,0:T(2,128)} %val_hbm.1, f32[2,512]{1,0:T(2,128)} %err_hbm.1, s32[2,32]{1,0:T(2,128)} %lvl_hbm.1), custom_call_target="tpu_custom_call" | custom-call | tf_op jit(solution)/shard_map/pallas_call | solution.py:493
  48.4 0.7 %copy.9 = f32[16,4096]{1,0:T(8,128)} copy(f32[16,4096]{1,0:T(8,128)S(1)} %shard_map.73) | data formatting | bytes 524288

commit v5 on v4

--- a/solution.py
+++ b/solution.py
@@ -187,25 +187,25 @@
 def transform(m_ref, amat, eye, stops):
     scal = jnp.sum(jnp.sum(amat * eye, axis=1, keepdims=True), axis=0, keepdims=True)
     m_ref[...] = amat
-    steps = amat.shape[0] // PIVOTS
-    most = NSIT - 2
-
-    def three(i, carry):
-        for k in range(3):
-            sweep(m_ref, (i * 3 + k) * PIVOTS)
-        return newton(eye, *carry)
-
-    def one(i, carry):
-        sweep(m_ref, (steps - NSIT + i) * PIVOTS)
-        return newton(eye, *carry)
+    most = amat.shape[0] // PIVOTS - 2 * NSIT
+
+    def several(count, offset):
+        def step(i, carry):
+            for k in range(count):
+                sweep(m_ref, (i * count + k + offset) * PIVOTS)
+            return newton(eye, *carry)
+
+        return step
 
     carry, done = (amat / scal, eye), 0
-    for stop, act in stops:
-        carry = lax.fori_loop(done, stop, three, carry)
+    for stop, act in stops + [(NSIT, lambda: None)]:
+        if done < most:
+            carry = lax.fori_loop(done, min(stop, most), several(3, 0), carry)
+        if stop > most:
+            carry = lax.fori_loop(max(done, most), stop, several(2, most), carry)
         act()
         done = stop
-    carry = lax.fori_loop(done, most, three, carry)
-    _, z = lax.fori_loop(most, NSIT, one, carry)
+    _, z = carry
     return z * lax.rsqrt(scal)
 
 
@@ -243,9 +243,9 @@
     twin = (cell + 1 - 2 * core, my)
 
     barrier = pltpu.get_barrier_semaphore()
-    for d in FAR_FIRST:
-        for peer in (z_peer(d), xc_peer(d), y_peer(d)):
-            pl.semaphore_signal(barrier, inc=1, device_id=peer, device_id_type=MESH)
+    for peer_of in (z_peer, y_peer, xc_peer):
+        for d in FAR_FIRST:
+            pl.semaphore_signal(barrier, inc=1, device_id=peer_of(d), device_id_type=MESH)
 
     pairs = [
         (own_hbm, own_ref), (blk_hbm, blk_ref), (gw_hbm.at[0], gw_ref.at[0]), (ens_hbm, ens_ref),
@@ -402,6 +402,7 @@
             c.start()
         grid_ref[b, mxc] = line_ref[b]
     forward(2, 0)
+    forward(2, 1)
     for c in c2[0]:
         c.wait_recv()
     packed(0)
@@ -417,26 +418,25 @@
             level = lvl_ref[b, k].astype(F32) * 0.25
             taper_ref[b : b + 1, k * 128 : (k + 1) * 128] = jnp.full((1, 128), level, F32)
     onward(0, NEAR[:4])
-    forward(2, 1)
     onward(0, NEAR[4:])
     for c in c3[1] + c6[1][:1]:
         c.start()
     for c in c6[0]:
         c.wait_recv()
 
-    def at_1_2():
+    def at_1_1():
         forward(3, 0)
 
-    def at_1_7():
+    def at_1_5():
         forward(3, 1)
 
     def at_1_9():
         onward(1, NEAR)
 
-    def at_2_2():
+    def at_1_10():
         forward(4, 0)
 
-    stops = [[(2, at_1_2), (7, at_1_7), (9, at_1_9)], [(2, at_2_2)]]
+    stops = [[(1, at_1_1), (5, at_1_5), (9, at_1_9), (10, at_1_10)], []]
 
     def prior_of(b):
         return jnp.concatenate([prior_ref[b, h] for h in range(NCORE)], axis=1)

time: 49.2 us -> 47.9 us (0.974)
  Pallas kernels: 48.3 us -> 47.1 us
    pallas_call x1, Pallas kernels: 48.3 us -> 47.1 us  [local(): pl.pallas_call(kernel, out_shape=pltpu.VMEM((members, cells), F32), in_sp...]
where the time goes in v5:
time: 47.9 us; the launch traced here: 47.8 us
  Pallas kernels  47.1 us (98%)
  local copies, waits for them, and re-layouts  0.71 us (1%)
    pallas_call x1, Pallas kernels, local(): pl.pallas_call(kernel, out_shape=pltpu.VMEM((members, cells), F32), in_sp...  47.1 us

profile of v5, /device:TPU:1, one launch (start us, length us, event | category | flops | bytes accessed | tf_op | source)
XLA Modules:
  0.0 47.8 jit_solution(17923770385408598375)
XLA Ops:
  0.0 47.1 %shard_map.73 = f32[16,4096]{1,0:T(8,128)S(1)} custom-call(f32[16,4096]{1,0:T(8,128)} %ens_hbm.1, s32[2,1,512]{2,1,0:T(1,128)} %bitcast.1, s32[2,512]{1,0:T(2,128)} %blk_hbm.1, f32[2,512,128]{2,1,0:T(8,128)} %gw_hbm.1, f32[2,512]{1,0:T(2,128)} %val_hbm.1, f32[2,512]{1,0:T(2,128)} %err_hbm.1, s32[2,32]{1,0:T(2,128)} %lvl_hbm.1), custom_call_target="tpu_custom_call" | custom-call | tf_op jit(solution)/shard_map/pallas_call | solution.py:493
  47.1 0.7 %copy.9 = f32[16,4096]{1,0:T(8,128)} copy(f32[16,4096]{1,0:T(8,128)S(1)} %shard_map.73) | data formatting | bytes 524288

commit v6 on v5

--- a/solution.py
+++ b/solution.py
@@ -74,24 +74,23 @@
     return (r >> 3) * (NXC * NZ) + tile, r & 7
 
 
-def compact(grid3, row, group, members):
-    count = row.shape[0]
-    lanes = iota((count, 128), 1)
+def selectors(row, group, members):
+    lanes = iota((row.shape[0], 128), 1)
+    held = 3 * NXC * NZ
     onehot = jnp.concatenate(
-        [
-            jnp.where(row == lanes + t * 128, 1.0, 0.0).astype(BF16)
-            for t in range(pl.cdiv(grid3.shape[0], 128))
-        ],
+        [jnp.where(row == lanes + t * 128, 1.0, 0.0).astype(BF16) for t in range(pl.cdiv(held, 128))],
         axis=1,
-    )[:, : grid3.shape[0]]
+    )[:, :held]
+    fold = jnp.where((iota((members, 384), 1) & 15) == iota((members, 384), 0), 1.0, 0.0)
+    return onehot, jnp.where((lanes >> 4) == group, 1.0, 0.0), fold.astype(BF16)
+
+
+def compact(grid3, onehot, keep, fold):
     picked = nn(onehot, grid3)
-    keep = (lanes >> 4) == group
     kept = jnp.concatenate(
-        [jnp.where(keep, picked[:, t * 128 : (t + 1) * 128], 0.0).astype(BF16) for t in range(3)],
-        axis=1,
+        [(keep * picked[:, t * 128 : (t + 1) * 128]).astype(BF16) for t in range(3)], axis=1
     )
-    fold = jnp.where((iota((members, 384), 1) & 15) == iota((members, 384), 0), 1.0, 0.0)
-    return nt(fold.astype(BF16), kept)
+    return nt(fold, kept)
 
 
 def gauge_taper(levels, o_row, b_row):
@@ -141,11 +140,11 @@
     return joined(nn(hq, wy)), joined(nn(hq, wz))
 
 
-def sweep(m_ref, j):
+def sweep(m_ref, j, low):
     n = m_ref.shape[0]
     span = range(PIVOTS)
     lane = iota((1, n), 1)
-    m = m_ref[...]
+    m = m_ref[low:, :]
     rows = [m_ref[pl.ds(j + i, 1), :] for i in span]
     at = [lane == j + i for i in span]
     e = [[None] * PIVOTS for _ in span]
@@ -179,7 +178,7 @@
     new = jnp.where(pivot, 0.0, m)
     for i in span:
         new = new - cols[i] * u[i]
-    m_ref[...] = new
+    m_ref[low:, :] = new
     for i in span:
         m_ref[pl.ds(j + i, 1), :] = u[i]
 
@@ -187,12 +186,13 @@
 def transform(m_ref, amat, eye, stops):
     scal = jnp.sum(jnp.sum(amat * eye, axis=1, keepdims=True), axis=0, keepdims=True)
     m_ref[...] = amat
-    most = amat.shape[0] // PIVOTS - 2 * NSIT
-
-    def several(count, offset):
+    half = amat.shape[0] // 2
+    most = half // (2 * PIVOTS)
+
+    def several(count, low):
         def step(i, carry):
             for k in range(count):
-                sweep(m_ref, (i * count + k + offset) * PIVOTS)
+                sweep(m_ref, low + ((i - (most if low else 0)) * count + k) * PIVOTS, low)
             return newton(eye, *carry)
 
         return step
@@ -200,13 +200,23 @@
     carry, done = (amat / scal, eye), 0
     for stop, act in stops + [(NSIT, lambda: None)]:
         if done < most:
-            carry = lax.fori_loop(done, min(stop, most), several(3, 0), carry)
+            carry = lax.fori_loop(done, min(stop, most), several(2, 0), carry)
         if stop > most:
-            carry = lax.fori_loop(max(done, most), stop, several(2, most), carry)
+            carry = lax.fori_loop(max(done, most), stop, several(4, half), carry)
         act()
         done = stop
     _, z = carry
     return z * lax.rsqrt(scal)
+
+
+def solved(m_ref, eye, bvec):
+    half = m_ref.shape[0] // 2
+    b_row = jnp.sum(eye * bvec, axis=0, keepdims=True)
+    second = -jnp.sum(m_ref[half:, :] * b_row, axis=1, keepdims=True)
+    second_row = jnp.sum(eye[half:] * second, axis=0, keepdims=True)
+    mixed = jnp.where(iota(b_row.shape, 1) < half, b_row, second_row)
+    first = -jnp.sum(m_ref[:half, :] * mixed, axis=1, keepdims=True)
+    return second_row + jnp.sum(eye[:half] * first, axis=0, keepdims=True)
 
 
 def apply_mix(mixer, x, taper):
@@ -264,6 +274,8 @@
         row_ref[b], group_ref[b] = places(o_col, rank_col)
         mine = (o_row == cell) & (rank_row.astype(I32) == slot)
         pick = jnp.where(mine, 1.0, 0.0).astype(BF16)
+        if b == 0:
+            staged[2].wait()
         g0, g1, g2 = split3(gw_ref[b])
         w_ref[...] = nn(pick, g0) + nn(pick, g1) + nn(pick, g2)
         blocks = jnp.broadcast_to(blk_ref[b : b + 1, :], (128, gauges)).astype(F32).astype(BF16)
@@ -294,7 +306,7 @@
                 tile = jnp.where((sub == 3) & (lane == k), level, tile)
         tile_ref[b] = tile
 
-    for c in staged[:3]:
+    for c in staged[:2]:
         c.wait()
     readings(0)
     for c in staged[4:]:
@@ -382,13 +394,14 @@
         for b in range(NBATCH)
     ]
 
-    def packed(b):
+    def choice(b):
+        mine = pl.ds(pl.multiple_of(core * half, half), half)
+        return selectors(row_ref[b, mine, :], group_ref[b, mine, :], members)
+
+    def packed(b, chosen):
         parts = [grid_ref[b, :, :, r, :].reshape(NXC * NZ, 128) for r in range(3)]
         grid3 = jnp.concatenate(split3(jnp.concatenate(parts, axis=0)), axis=1)
-        mine = pl.ds(pl.multiple_of(core * half, half), half)
-        prior_ref[b, core, rows(my), :] = compact(
-            grid3, row_ref[b, mine, :], group_ref[b, mine, :], members
-        )
+        prior_ref[b, core, rows(my), :] = compact(grid3, *chosen)
 
     def onward(b, ranks):
         for k in ranks:
@@ -401,16 +414,17 @@
         for c in c2[b]:
             c.start()
         grid_ref[b, mxc] = line_ref[b]
+    chosen = choice(0)
     forward(2, 0)
     forward(2, 1)
     for c in c2[0]:
         c.wait_recv()
-    packed(0)
+    packed(0, chosen)
     for c in c3[0] + c6[0][:1]:
         c.start()
     for c in c2[1]:
         c.wait_recv()
-    packed(1)
+    packed(1, choice(1))
     levels = grid_ref[1, :, :, 3, :].reshape(NXC * NZ, 128)
     taper_g = gauge_taper(levels, own_ref[1], blk_ref[1:2, :])
     for b in range(NBATCH):
@@ -421,22 +435,18 @@
     onward(0, NEAR[4:])
     for c in c3[1] + c6[1][:1]:
         c.start()
+    forward(3, 0)
     for c in c6[0]:
         c.wait_recv()
 
-    def at_1_1():
-        forward(3, 0)
-
-    def at_1_5():
+    def at_1_4():
         forward(3, 1)
 
     def at_1_9():
         onward(1, NEAR)
-
-    def at_1_10():
         forward(4, 0)
 
-    stops = [[(1, at_1_1), (5, at_1_5), (9, at_1_9), (10, at_1_10)], []]
+    stops = [[(4, at_1_4), (9, at_1_9)], []]
 
     def prior_of(b):
         return jnp.concatenate([prior_ref[b, h] for h in range(NCORE)], axis=1)
@@ -449,7 +459,7 @@
         gram, bvec = innovations(prior, val_ref[b : b + 1, :], err_ref[b : b + 1, :])
         amat = eye + gram
         dmat = transform(m_ref, amat, eye, stops[b]) - eye
-        w_row = -jnp.sum(m_ref[...] * bvec, axis=0, keepdims=True)
+        w_row = solved(m_ref, eye, bvec)
         mixer = dmat + w_row * scale
         mix_ref[b] = mixer
         if b == 0:

time: 47.9 us -> 47.4 us (0.990)
  Pallas kernels: 47.1 us -> 46.5 us
    pallas_call x1, Pallas kernels: 47.1 us -> 46.5 us  [local(): pl.pallas_call(kernel, out_shape=pltpu.VMEM((members, cells), F32), in_sp...]
where the time goes in v6:
time: 47.4 us; the launch traced here: 47.2 us
  Pallas kernels  46.5 us (98%)
  local copies, waits for them, and re-layouts  0.71 us (1%)
    pallas_call x1, Pallas kernels, local(): pl.pallas_call(kernel, out_shape=pltpu.VMEM((members, cells), F32), in_sp...  46.5 us

profile of v6, /device:TPU:1, one launch (start us, length us, event | category | flops | bytes accessed | tf_op | source)
XLA Modules:
  0.0 47.2 jit_solution(16445255552973772314)
XLA Ops:
  0.0 46.5 %shard_map.73 = f32[16,4096]{1,0:T(8,128)S(1)} custom-call(f32[16,4096]{1,0:T(8,128)} %ens_hbm.1, s32[2,1,512]{2,1,0:T(1,128)} %bitcast.1, s32[2,512]{1,0:T(2,128)} %blk_hbm.1, f32[2,512,128]{2,1,0:T(8,128)} %gw_hbm.1, f32[2,512]{1,0:T(2,128)} %val_hbm.1, f32[2,512]{1,0:T(2,128)} %err_hbm.1, s32[2,32]{1,0:T(2,128)} %lvl_hbm.1), custom_call_target="tpu_custom_call" | custom-call | tf_op jit(solution)/shard_map/pallas_call | solution.py:503
  46.5 0.7 %copy.9 = f32[16,4096]{1,0:T(8,128)} copy(f32[16,4096]{1,0:T(8,128)S(1)} %shard_map.73) | data formatting | bytes 524288

commit v7 on v6

--- a/solution.py
+++ b/solution.py
@@ -104,11 +104,11 @@
     return jnp.sum(jnp.where(hit, by_block, 0.0), axis=0, keepdims=True)
 
 
-def innovations(prior, value, error):
+def innovations(prior, shift, value, error):
     members = prior.shape[0]
     ymean = jnp.sum(prior, axis=0, keepdims=True) / members
     smat = (prior - ymean) * (1.0 / (error * jnp.sqrt(jnp.float32(members - 1))))
-    dvec = (value - ymean) / error
+    dvec = (value - (ymean + shift)) / error
     sh, sl = split2(smat)
     both = jnp.concatenate([sh, sl], axis=0)
     top = nt(sh, both)
@@ -216,7 +216,8 @@
     second_row = jnp.sum(eye[half:] * second, axis=0, keepdims=True)
     mixed = jnp.where(iota(b_row.shape, 1) < half, b_row, second_row)
     first = -jnp.sum(m_ref[:half, :] * mixed, axis=1, keepdims=True)
-    return second_row + jnp.sum(eye[:half] * first, axis=0, keepdims=True)
+    row = second_row + jnp.sum(eye[:half] * first, axis=0, keepdims=True)
+    return row, jnp.concatenate([first, second], axis=0)
 
 
 def apply_mix(mixer, x, taper):
@@ -454,19 +455,22 @@
     total = members * NY
     eye = jnp.where(iota((total, total), 0) == iota((total, total), 1), 1.0, 0.0)
     scale = 1.0 / jnp.sqrt(jnp.float32(total - 1))
-    prior = prior_of(0)
+    prior, shift = prior_of(0), 0.0
     for b in range(NBATCH):
-        gram, bvec = innovations(prior, val_ref[b : b + 1, :], err_ref[b : b + 1, :])
+        gram, bvec = innovations(prior, shift, val_ref[b : b + 1, :], err_ref[b : b + 1, :])
         amat = eye + gram
         dmat = transform(m_ref, amat, eye, stops[b]) - eye
-        w_row = solved(m_ref, eye, bvec)
+        w_row, w_col = solved(m_ref, eye, bvec)
         mixer = dmat + w_row * scale
         mix_ref[b] = mixer
         if b == 0:
             for c in c6[1]:
                 c.wait_recv()
             centred = mixer - jnp.sum(mixer, axis=0, keepdims=True) / total
-            prior = apply_mix(mixer, prior_of(1), taper_g)
+            before = prior_of(1)
+            prior = apply_mix(dmat, before, taper_g)
+            apart = before - jnp.sum(before, axis=0, keepdims=True) / total
+            shift = taper_g * (scale * jnp.sum(w_col * apart, axis=0, keepdims=True))
     own = [mix_ref[b, rows(my), :] for b in range(NBATCH)]
     stack = jnp.concatenate(own + [wide(own[1], centred)], axis=0)
     hi, lo = split2(stack)

time: 47.4 us -> 47.4 us (level)
  no operation moved by 1% of the time
where the time goes in v7:
time: 47.4 us; the launch traced here: 47.2 us
  Pallas kernels  46.5 us (98%)
  local copies, waits for them, and re-layouts  0.71 us (1%)
    pallas_call x1, Pallas kernels, local(): pl.pallas_call(kernel, out_shape=pltpu.VMEM((members, cells), F32), in_sp...  46.5 us

profile of v7, /device:TPU:1, one launch (start us, length us, event | category | flops | bytes accessed | tf_op | source)
XLA Modules:
  0.0 47.2 jit_solution(14753149463178084568)
XLA Ops:
  0.0 46.5 %shard_map.73 = f32[16,4096]{1,0:T(8,128)S(1)} custom-call(f32[16,4096]{1,0:T(8,128)} %ens_hbm.1, s32[2,1,512]{2,1,0:T(1,128)} %bitcast.1, s32[2,512]{1,0:T(2,128)} %blk_hbm.1, f32[2,512,128]{2,1,0:T(8,128)} %gw_hbm.1, f32[2,512]{1,0:T(2,128)} %val_hbm.1, f32[2,512]{1,0:T(2,128)} %err_hbm.1, s32[2,32]{1,0:T(2,128)} %lvl_hbm.1), custom_call_target="tpu_custom_call" | custom-call | tf_op jit(solution)/shard_map/pallas_call | solution.py:507
  46.5 0.7 %copy.9 = f32[16,4096]{1,0:T(8,128)} copy(f32[16,4096]{1,0:T(8,128)S(1)} %shard_map.73) | data formatting | bytes 524288
